TPU v7x, 32 devices: a whole 2x2x4 slice. The times are simulated.
32 devices in a mesh: ctx: 4 (over y, x), exp: 8 (over z, core).
Axes of the slice: x: 2, y: 2, z: 4, core: 2. Of those that a mesh axis runs over, the one named last changes fastest.
Arguments:
- query: bfloat16 [8, 256, 2048], P('exp', 'ctx'), may hold values from -24 to 24
- key_value: bfloat16 [8, 256, 2, 256], P('exp', 'ctx'), may hold values from -24 to 24
- positions: int32 [8, 256], P('exp', 'ctx'), may hold values from 0 to 255, as said below
- resid: bfloat16 [8, 256, 1440], P('exp', 'ctx'), may hold values from -6 to 6
- sinks: float32 [32], replicated, may hold values from -2 to 3
- o_weight: bfloat16 [2048, 1440], P('exp'), may hold values from -0.125 to 0.125
- norm_gain: float32 [1440], replicated, may hold values from 0.25 to 1.75
- expert_ids: int32 [8, 256, 4], P('exp', 'ctx'), may hold values from 0 to 7, all different within a row; in each aligned block of 64 rows (0 to 63, 64 to 127, ..., all dimensions but the last counted through in order) at most 32 rows name the same one
- route_weights: float32 [8, 256, 4], P('exp', 'ctx'), may hold values from 0.1 to 0.5
- w_gate: bfloat16 [1440, 11520], P(None, ('ctx', 'exp')), may hold values from -0.15625 to 0.15625
- w_up: bfloat16 [1440, 11520], P(None, ('ctx', 'exp')), may hold values from -0.15625 to 0.15625
- w_down: bfloat16 [11520, 1440], P(('ctx', 'exp')), may hold values from -0.15625 to 0.15625
Outputs:
- out: bfloat16 [8, 256, 1440], P('exp', 'ctx')
Inputs may be any that keep to these rules, and one draw needn't show every extreme that they name: Within each sequence every position appears once; the 64 stored rows of one device are two runs of 32 consecutive ascending positions, each run starting at a multiple of 32. `expert_ids`: each row names 4 different experts; among the 64 rows of one device no expert is named more than 32 times, a bound that some block reaches.
All inputs are finite; a program needn't handle non-finite values.
Results may differ from a plain program's by a relative error of at most 0.0075.
Values may be sent and summed in bfloat16 or wider, within the bound.
A program may use at most 64 MiB of HBM per device.

v0:
```python
import math

import jax
import jax.numpy as jnp
from jax import lax
from jax.sharding import PartitionSpec as P

D = 1440
QH = 32
KVH = 4
HD = 64
TOP = 4
SLICES = 4


NEG_FILL = -1e30


def passed_along(value, axis, by):
    length = lax.axis_size(axis)
    return lax.ppermute(value, axis, [(i, (i + by) % length) for i in range(length)])


def from_partner(block, axis, bit):
    count = lax.axis_size(axis)
    route = []
    for low in range(count):
        high = low | 1 << bit
        if high != low and high < count:
            route += [(low, high), (high, low)]
    return lax.ppermute(block, axis, route)


def attend_block(grouped, keys, values, query_pos, key_pos, state):
    run_max, run_sum, accum = state
    scores = jnp.einsum("rgjd,sgd->gjrs", grouped, keys, preferred_element_type=jnp.float32) * (
        1.0 / math.sqrt(HD)
    )
    allowed = key_pos[None, :] <= query_pos[:, None]
    scores = jnp.where(allowed[None, None], scores, NEG_FILL)
    new_max = jnp.maximum(run_max, jnp.max(scores, axis=-1))
    factor = jnp.exp(run_max - new_max)
    weights = jnp.exp(scores - new_max[..., None])
    run_sum = run_sum * factor + jnp.sum(weights, axis=-1)
    accum = accum * factor[..., None] + jnp.einsum(
        "gjrs,sgd->gjrd", weights, values.astype(jnp.float32), precision=lax.Precision.HIGHEST
    )
    return (new_max, run_sum, accum)


def body(
    query,
    key_value,
    positions,
    resid,
    sinks,
    o_weight,
    norm_gain,
    expert_ids,
    route_weights,
    w_gate,
    w_up,
    w_down,
):
    rows = query.shape[1]
    group = QH // KVH
    grouped = query[0].reshape(rows, KVH, group, HD)
    own_kv = key_value[0]
    own_pos = positions[0]
    start_max = jnp.broadcast_to(sinks.reshape(KVH, group)[:, :, None], (KVH, group, rows))
    state = (
        start_max,
        jnp.ones((KVH, group, rows), jnp.float32),
        jnp.zeros((KVH, group, rows, HD), jnp.float32),
    )

    def take(block, block_pos, carry):
        width = block.shape[0]
        keys = block[:, 0].reshape(width, KVH, HD)
        values = block[:, 1].reshape(width, KVH, HD)
        return attend_block(grouped, keys, values, own_pos, block_pos, carry)

    state = take(own_kv, own_pos, state)

    def turn(step, carry):
        block, block_pos, inner = carry
        block, block_pos = passed_along((block, block_pos), "ctx", 1)
        return (block, block_pos, take(block, block_pos, inner))

    state = lax.fori_loop(0, lax.axis_size("ctx") - 1, turn, (own_kv, own_pos, state))[2]
    run_max, run_sum, accum = state
    attended = accum / run_sum[..., None]
    attended = jnp.transpose(attended, (2, 0, 1, 3)).reshape(rows, QH * HD).astype(jnp.bfloat16)
    projected = jnp.dot(
        attended,
        lax.all_gather(o_weight, "exp", axis=0, tiled=True),
        preferred_element_type=jnp.float32,
    )
    mixed = resid[0].astype(jnp.float32) + projected
    normed = (
        mixed * lax.rsqrt(jnp.mean(mixed * mixed, axis=-1, keepdims=True) + 1e-05) * norm_gain
    ).astype(jnp.bfloat16)
    n_ctx = lax.axis_size("ctx")
    n_exp = lax.axis_size("exp")
    n_experts = n_ctx * n_exp // SLICES
    per_row = n_exp // SLICES
    cap = max(2, rows * TOP // n_experts)
    n_slots = n_experts * cap
    chosen = expert_ids[0].reshape(rows * TOP)
    onehot = (chosen[:, None] == jnp.arange(n_experts, dtype=jnp.int32)[None, :]).astype(jnp.int32)
    rank = jnp.sum((jnp.cumsum(onehot, axis=0) - onehot) * onehot, axis=1)
    slot = (chosen % per_row * n_ctx + chosen // per_row) * cap + rank
    source = (
        jnp.zeros((n_slots,), jnp.int32)
        .at[slot]
        .set(jnp.arange(rows * TOP, dtype=jnp.int32) // TOP)
    )
    filled = jnp.zeros((n_slots,), jnp.bool_).at[slot].set(True)
    outgoing = jnp.where(filled[:, None], normed[source], jnp.zeros((), jnp.bfloat16)).reshape(
        per_row, n_ctx, cap, D
    )
    arrived = lax.all_to_all(outgoing, "ctx", split_axis=1, concat_axis=1, tiled=True)
    pieces = arrived.reshape(n_exp, n_ctx // SLICES, cap, D)
    held = lax.all_to_all(pieces, "exp", split_axis=0, concat_axis=0, tiled=True)
    place = lax.axis_index("exp")
    for bit in range(SLICES.bit_length() - 1):
        partner = from_partner(held, "exp", bit)
        upper = place >> bit & 1 == 1
        held = jnp.where(
            upper,
            jnp.concatenate([partner, held], axis=1),
            jnp.concatenate([held, partner], axis=1),
        )
    flat = held.reshape(-1, D)
    gate = jnp.dot(flat, w_gate, preferred_element_type=jnp.float32)
    lifted = jnp.dot(flat, w_up, preferred_element_type=jnp.float32)
    active = (gate * jax.nn.sigmoid(1.702 * gate) * (lifted + 1.0)).astype(jnp.bfloat16)
    back = lax.all_to_all(
        jnp.dot(active, w_down, preferred_element_type=jnp.float32)
        .astype(jnp.bfloat16)
        .reshape(held.shape),
        "exp",
        split_axis=0,
        concat_axis=0,
        tiled=True,
    )
    count = back.shape[1]
    summed = jnp.sum(back.reshape(per_row, SLICES, count, cap, D).astype(jnp.float32), axis=1)
    result = summed.astype(jnp.bfloat16)
    returned = lax.all_to_all(result, "ctx", split_axis=1, concat_axis=1, tiled=True)
    picked = returned.reshape(n_slots, D)[slot].astype(jnp.float32).reshape(rows, TOP, D)
    final = mixed + jnp.sum(route_weights[0][:, :, None] * picked, axis=1)
    return final.astype(jnp.bfloat16)[None]


def solution(mesh):
    return jax.shard_map(
        body,
        mesh=mesh,
        in_specs=(
            P("exp", "ctx", None),
            P("exp", "ctx", None, None),
            P("exp", "ctx"),
            P("exp", "ctx", None),
            P(),
            P("exp", None),
            P(),
            P("exp", "ctx", None),
            P("exp", "ctx", None),
            P(None, ("ctx", "exp")),
            P(None, ("ctx", "exp")),
            P(("ctx", "exp"), None),
        ),
        out_specs=P("exp", "ctx", None),
        check_vma=False,
    )
```

profile of v0, /device:TPU:0, one launch (start us, length us, event | category | flops | bytes accessed | tf_op | source)
XLA Modules:
  0.0 281.3 jit_solution(7892060236818463822)
XLA Ops:
  6.5 0.7 all-gather.2.cloned.1.call-update
  7.3 0.8 copy.79
  8.4 0.9 copy.121
  9.3 1.5 reshape_squeeze.13
  11.3 0.7 fusion.34
  12.4 1.2 convolution_add_fusion.2
  13.5 28.3 %while.18 = (s32[]{:T(128)}, bf16[64,2,256]{2,0,1:T(8,128)(2,1)S(1)}, s32[64]{0:T(128)S(1)}, f32[4,8,64]{2,1,0:T(8,128)S(1)}, f32[4,8,64]{2,1,0:T(8,128)S(1)}, /...) while((s32[]{:T(128)}, ...), condition=%wide.region_5.6_spmd, body=%wide.region_2.5_spmd.sunk | while | flops 118759424 | bytes 3754157 | solution.py:90
  13.6 3.0 %collective-permute-start.1 = (s32[64]{0:T(128)S(1)}, s32[64]{0:T(128)S(1)}, u32[]{:S(2)}, u32[]{:S(2)}) collective-permute-start(s32[64]{0:T(128)S(1)} %get-tuple-element.184), channel_id=1, source_target_pairs={{0,8},{8,16},{16,24},{24,0},{1,9},{9,17},{17,25},{25,1},{2,10},{10... | collective-permute-start | bytes 776 | tf_op jit(solution)/shard_map/while/body/eval_jaxpr/ppermute | solution.py:21
  16.5 1.5 collective-permute-start
  18.0 1.0 collective-permute-done.1
  19.1 2.6 collective-permute-done
  22.9 1.3 convolution_add_fusion.4
  24.3 0.6 collective-permute-start.1
  24.9 2.4 collective-permute-start
  27.3 1.5 collective-permute-done.1
  28.8 1.2 collective-permute-done
  30.3 0.6 select_reduce_fusion.2
  31.2 1.3 convolution_add_fusion.4
  32.6 1.5 collective-permute-start.1
  34.2 1.0 collective-permute-start
  35.1 2.0 collective-permute-done.1
  37.2 2.1 collective-permute-done
  39.6 0.6 select_reduce_fusion.2
  40.5 1.3 convolution_add_fusion.4
  44.0 1.4 scatter_custom_fusion.1
  45.4 1.5 scatter_custom_fusion
  47.1 26.5 %all-gather.2.cloned.1.call-done = bf16[2048,1440]{0,1:T(8,128)(2,1)} async-done(((bf16[256,1440]{0,1:T(8,128)(2,1)}), bf16[2048,1440]{0,1:T(8,128)(2,1)}) %all-gather.2.cloned.1.call-update) | async-done | bytes 5898256 | tf_op jit(solution)/shard_map/all_gather | solution.py:96
  73.6 4.7 %multiply_reduce_fusion.1 = (f32[64]{0:T(128)S(1)}, f32[64,1440]{1,0:T(8,128)S(1)}) fusion(bf16[64,2048]{1,0:T(8,128)(2,1)S(1)} %convert_element_type.49, bf16[2048,1440]{0,1:T(8,128)(2,1)} %all-gather.2.cloned.1.call-done, bf16[1,64,1440]{2,1,0:T(8,128)(2,1)S(1)} %copy-done.3), kind=kOutput, calls=%fused_computation.40 | convolution fusion | flops 377855936 | bytes 6713600 | tf_op jit(solution)/shard_map/dot_general | solution.py:94
  78.4 1.3 gather_fusion
  79.8 15.2 %all_to_all.20 = bf16[2,4,32,1440]{3,2,0,1:T(8,128)(2,1)S(1)} all-to-all(bf16[2,4,32,1440]{3,2,0,1:T(8,128)(2,1)S(1)} %copy_select_fusion), channel_id=1, replica_groups=mesh['ctx'=4,'exp'=8] {'ctx'}, dimensions={1} | all-to-all | bytes 1474560 | tf_op jit(solution)/shard_map/all_to_all | solution.py:122
  95.1 23.4 %all_to_all.21 = bf16[8,1,32,1440]{3,2,1,0:T(8,128)(2,1)S(1)} all-to-all(bf16[8,1,32,1440]{3,2,1,0:T(8,128)(2,1)S(1)} %bitcast.74), channel_id=1, replica_groups=mesh['ctx'=4,'exp'=8] {'exp'}, dimensions={0} | all-to-all | bytes 1474560 | tf_op jit(solution)/shard_map/all_to_all | solution.py:124
  118.5 0.9 copy-done.2
  119.4 1.5 collective-permute-done.2
  120.9 2.1 maximum_select_fusion.1
  123.1 36.5 %collective-permute-done.3 = bf16[8,2,32,1440]{3,2,1,0:T(8,128)(2,1)} collective-permute-done((bf16[8,2,32,1440]{3,2,1,0:T(8,128)(2,1)S(1)}, bf16[8,2,32,1440]{3,2,1,0:T(8,128)(2,1)}, u32[]{:S(2)}, u32[]{:S(2)}) %collective-permute-start.3) | collective-permute-done | bytes 1474592 | tf_op jit(solution)/shard_map/ppermute | solution.py:31
  159.7 2.6 maximum_select_fusion
  162.2 1.7 copy-done.1
  163.9 2.5 fusion.35
  166.4 7.0 %convolution_convert_fusion = bf16[1024,1440]{0,1:T(8,128)(2,1)} fusion(bf16[360,1440]{1,0:T(8,128)(2,1)S(1)} %copy-done, f32[1024,360]{0,1:T(8,128)} %fusion.35, bf16[1024,1440]{1,0:T(8,128)(2,1)} %bitcast.73, bf16[1440,360]{1,0:T(8,128)(2,1)S(1)} %copy-done.9), kind=kOutput, calls=%fused_computation.19 | convolution fusion | flops 2127790080 | bytes 9446400 | tf_op jit(solution)/shard_map/dot_general | solution.py:139
  173.4 4.6 %copy.86 = bf16[1024,1440]{1,0:T(8,128)(2,1)} copy(bf16[1024,1440]{0,1:T(8,128)(2,1)} %convolution_convert_fusion) | data formatting | bytes 5898240 | tf_op jit(solution)/shard_map/convert_element_type | solution.py:140
  178.0 75.1 %all_to_all.22 = bf16[8,4,32,1440]{3,2,1,0:T(8,128)(2,1)S(1)} all-to-all(bf16[8,4,32,1440]{3,2,1,0:T(8,128)(2,1)} %bitcast.69), channel_id=1, replica_groups=mesh['ctx'=4,'exp'=8] {'exp'}, dimensions={0} | all-to-all | bytes 5898240 | tf_op jit(solution)/shard_map/all_to_all | solution.py:138
  253.6 0.9 copy.87
  254.6 3.5 %all-to-all-start.3 = ((bf16[2,4,32,1440]{3,2,0,1:T(8,128)(2,1)}), bf16[2,4,32,1440]{3,2,0,1:T(8,128)(2,1)S(1)}, u32[]{:S(2)}, u32[]{:S(2)}) async-start(bf16[2,4,32,1440]{3,2,0,1:T(8,128)(2,1)} %copy.87), calls=%async_computation.3 | async-start | bytes 1572864 | tf_op jit(solution)/shard_map/all_to_all | solution.py:150
  258.2 10.6 %all-to-all-done.3 = bf16[2,4,32,1440]{3,2,0,1:T(8,128)(2,1)S(1)} async-done(((bf16[2,4,32,1440]{3,2,0,1:T(8,128)(2,1)}), bf16[2,4,32,1440]{3,2,0,1:T(8,128)(2,1)S(1)}, u32[]{:S(2)}, u32[]{:S(2)}) %all-to-all-start.3) | async-done | bytes 737312 | tf_op jit(solution)/shard_map/all_to_all | solution.py:150
  268.8 2.1 gather_fusion.1
  270.9 1.7 reshape.256
  272.7 1.1 multiply_reduce_fusion
  273.8 0.7 fusion.15
  (89 shorter events, 6.8 us)
Async XLA Ops:
  6.5 159.9 %copy-start = (bf16[360,1440]{1,0:T(8,128)(2,1)S(1)}, bf16[360,1440]{1,0:T(8,128)(2,1)}, u32[]{:S(2)}) copy-start(bf16[360,1440]{1,0:T(8,128)(2,1)} %param.25) | copy-start | bytes 3110404
  6.5 4.3 %copy-start.7 = (f32[32]{0:T(128)S(1)}, f32[32]{0:T(128)}, u32[]{:S(2)}) copy-start(f32[32]{0:T(128)} %param.18) | copy-start | bytes 388
  6.5 4.7 %copy-start.4 = (s32[1,64]{1,0:T(1,128)S(1)}, s32[1,64]{1,0:T(1,128)}, u32[]{:S(2)}) copy-start(s32[1,64]{1,0:T(1,128)} %param.16) | copy-start | bytes 772
  6.5 67.1 %all-gather.2.cloned.1.call-start = ((), (), s32[]{:S(2)}) async-start(), calls=%async_computation.4 | async-start | bytes 6635520 | tf_op jit(solution)/shard_map/all_gather | solution.py:96
  13.6 5.5 %collective-permute-start.1 = (s32[64]{0:T(128)S(1)}, s32[64]{0:T(128)S(1)}, u32[]{:S(2)}, u32[]{:S(2)}) collective-permute-start(s32[64]{0:T(128)S(1)} %get-tuple-element.184), channel_id=1, source_target_pairs={{0,8},{8,16},{16,24},{24,0},{1,9},{9,17},{17,25},{25,1},{2,10},{10... | collective-permute-start | bytes 776 | tf_op jit(solution)/shard_map/while/body/eval_jaxpr/ppermute | solution.py:21
  16.5 5.2 %collective-permute-start = (bf16[64,2,256]{2,0,1:T(8,128)(2,1)S(1)}, bf16[64,2,256]{2,0,1:T(8,128)(2,1)S(1)}, u32[]{:S(2)}, u32[]{:S(2)}) collective-permute-start(bf16[64,2,256]{2,0,1:T(8,128)(2,1)S(1)} %get-tuple-element.183), channel_id=1, source_target_pairs={{0,8},{8,16},{16,24},{24,0},{1,9},{9,17},{17,25},{25,1},{2,10},{10... | collective-permute-start | bytes 196616 | tf_op jit(solution)/shard_map/while/body/eval_jaxpr/ppermute | solution.py:21
  24.3 4.5 %collective-permute-start.1 = (s32[64]{0:T(128)S(1)}, s32[64]{0:T(128)S(1)}, u32[]{:S(2)}, u32[]{:S(2)}) collective-permute-start(s32[64]{0:T(128)S(1)} %get-tuple-element.184), channel_id=1, source_target_pairs={{0,8},{8,16},{16,24},{24,0},{1,9},{9,17},{17,25},{25,1},{2,10},{10... | collective-permute-start | bytes 776 | tf_op jit(solution)/shard_map/while/body/eval_jaxpr/ppermute | solution.py:21
  24.9 5.2 %collective-permute-start = (bf16[64,2,256]{2,0,1:T(8,128)(2,1)S(1)}, bf16[64,2,256]{2,0,1:T(8,128)(2,1)S(1)}, u32[]{:S(2)}, u32[]{:S(2)}) collective-permute-start(bf16[64,2,256]{2,0,1:T(8,128)(2,1)S(1)} %get-tuple-element.183), channel_id=1, source_target_pairs={{0,8},{8,16},{16,24},{24,0},{1,9},{9,17},{17,25},{25,1},{2,10},{10... | collective-permute-start | bytes 196616 | tf_op jit(solution)/shard_map/while/body/eval_jaxpr/ppermute | solution.py:21
  32.6 4.5 %collective-permute-start.1 = (s32[64]{0:T(128)S(1)}, s32[64]{0:T(128)S(1)}, u32[]{:S(2)}, u32[]{:S(2)}) collective-permute-start(s32[64]{0:T(128)S(1)} %get-tuple-element.184), channel_id=1, source_target_pairs={{0,8},{8,16},{16,24},{24,0},{1,9},{9,17},{17,25},{25,1},{2,10},{10... | collective-permute-start | bytes 776 | tf_op jit(solution)/shard_map/while/body/eval_jaxpr/ppermute | solution.py:21
  34.2 5.2 %collective-permute-start = (bf16[64,2,256]{2,0,1:T(8,128)(2,1)S(1)}, bf16[64,2,256]{2,0,1:T(8,128)(2,1)S(1)}, u32[]{:S(2)}, u32[]{:S(2)}) collective-permute-start(bf16[64,2,256]{2,0,1:T(8,128)(2,1)S(1)} %get-tuple-element.183), channel_id=1, source_target_pairs={{0,8},{8,16},{16,24},{24,0},{1,9},{9,17},{17,25},{25,1},{2,10},{10... | collective-permute-start | bytes 196616 | tf_op jit(solution)/shard_map/while/body/eval_jaxpr/ppermute | solution.py:21
  41.9 31.7 %copy-start.3 = (bf16[1,64,1440]{2,1,0:T(8,128)(2,1)S(1)}, bf16[1,64,1440]{2,1,0:T(8,128)(2,1)}, u32[]{:S(2)}) copy-start(bf16[1,64,1440]{2,1,0:T(8,128)(2,1)} %param.17) | copy-start | bytes 552964
  47.1 31.3 %copy-start.5 = (f32[1440]{0:T(1024)S(1)}, f32[1440]{0:T(1024)}, u32[]{:S(2)}) copy-start(f32[1440]{0:T(1024)} %param.20) | copy-start | bytes 17284
  118.5 0.9 copy-start.2
  118.5 2.4 collective-permute-start.2
  123.0 36.6 %collective-permute-start.3 = (bf16[8,2,32,1440]{3,2,1,0:T(8,128)(2,1)S(1)}, bf16[8,2,32,1440]{3,2,1,0:T(8,128)(2,1)}, u32[]{:S(2)}, u32[]{:S(2)}) collective-permute-start(bf16[8,2,32,1440]{3,2,1,0:T(8,128)(2,1)S(1)} %maximum_select_fusion.1), channel_id=1, source_target_pairs={{0,2},{2,0},{1,3},{3,1},{4,6},{6,4},{5,7},{7,5},{8,10},{10,8},{9,1... | collective-permute-start | bytes 4423688 | tf_op jit(solution)/shard_map/ppermute | solution.py:31
  123.1 40.8 %copy-start.8 = (bf16[1440,360]{1,0:T(8,128)(2,1)S(1)}, bf16[1440,360]{1,0:T(8,128)(2,1)}, u32[]{:S(2)}) copy-start(bf16[1440,360]{1,0:T(8,128)(2,1)} %param.23) | copy-start | bytes 3110404
  162.2 1.7 copy-start.1
  163.9 2.5 copy-start.9
  253.6 4.4 %copy-start.6 = (f32[1,64,4]{1,2,0:T(4,128)S(1)}, f32[1,64,4]{1,2,0:T(4,128)}, u32[]{:S(2)}) copy-start(f32[1,64,4]{1,2,0:T(4,128)} %param.22) | copy-start | bytes 3076
  254.6 14.2 %all-to-all-start.3 = ((bf16[2,4,32,1440]{3,2,0,1:T(8,128)(2,1)}), bf16[2,4,32,1440]{3,2,0,1:T(8,128)(2,1)S(1)}, u32[]{:S(2)}, u32[]{:S(2)}) async-start(bf16[2,4,32,1440]{3,2,0,1:T(8,128)(2,1)} %copy.87), calls=%async_computation.3 | async-start | bytes 1572864 | tf_op jit(solution)/shard_map/all_to_all | solution.py:150
Sparse Core Ops, SparseCore 0:
  9.0 64.6 all-gather.1
where the time goes:
time: 282 us; the launch traced here: 281 us
  blocking collectives  114 us (40%)
  waiting for transfers between devices  86.3 us (31%)
  matrix products  22 us (8%)
  local copies, waits for them, and re-layouts  21.9 us (8%)
  between operations  13.7 us (5%)
  starting transfers between devices  13.6 us (5%)
  other arithmetic  9.81 us (3%)
    all_to_all x1, blocking collectives, body(): lax.all_to_all(jnp.dot(active, w_down, preferred_element_type=jnp.float32...  75.1 us
    ppermute x2, waiting for transfers between devices, from_partner(): return lax.ppermute(block, axis, route)  38.1 us
    all_gather x1, waiting for transfers between devices, body(): lax.all_gather(o_weight, 'exp', axis=0, tiled=True)  26.5 us
    all_to_all x1, blocking collectives, body(): lax.all_to_all(pieces, 'exp', split_axis=0, concat_axis=0, tiled=True)  23.4 us
    all_to_all x1, blocking collectives, body(): lax.all_to_all(outgoing, 'ctx', split_axis=1, concat_axis=1, tiled=True)  15.2 us
    all_to_all x1, waiting for transfers between devices, body(): lax.all_to_all(result, 'ctx', split_axis=1, concat_axis=1, tiled=True)  10.6 us
    ppermute x6, waiting for transfers between devices, passed_along(): lax.ppermute(value, axis, [(i, (i + by) % length) for i in range(length)])  10.4 us
    ppermute x6, starting transfers between devices, passed_along(): lax.ppermute(value, axis, [(i, (i + by) % length) for i in range(length)])  10 us
  transfers between devices with their start and end apart: 10, of which 10 were waited for; matrix products, arithmetic and copies ran while one was open for 7% of the time, Pallas kernels for 0%

commit v1 on v0

v1 whole, which is shorter than its diff:
```python
import math

import jax
import jax.numpy as jnp
from jax import lax
from jax.sharding import PartitionSpec as P

D = 1440
QH = 32
KVH = 4
HD = 64
TOP = 4
SLICES = 4


NEG_FILL = -1e30


def passed_along(value, axis, by):
    length = lax.axis_size(axis)
    return lax.ppermute(value, axis, [(i, (i + by) % length) for i in range(length)])


def from_partner(block, axis, bit):
    count = lax.axis_size(axis)
    route = []
    for low in range(count):
        high = low | 1 << bit
        if high != low and high < count:
            route += [(low, high), (high, low)]
    return lax.ppermute(block, axis, route)


def attend(query, key_value, positions, sinks):
    rows = query.shape[0]
    group = QH // KVH
    width = KVH * HD
    coarse = (positions // 32).astype(jnp.bfloat16)[:, None]
    fine = (positions % 32).astype(jnp.bfloat16)[:, None]
    own = jnp.concatenate(
        [
            key_value.reshape(rows, 2 * width),
            coarse,
            fine,
            jnp.zeros((rows, 126), jnp.bfloat16),
        ],
        axis=1,
    )
    blocks = [own]
    for by in range(1, lax.axis_size("ctx")):
        blocks.append(passed_along(own, "ctx", by))
    whole = jnp.concatenate(blocks, axis=0)
    keys = whole[:, :width].reshape(-1, KVH, HD)
    values = whole[:, width : 2 * width].reshape(-1, KVH, HD)
    key_pos = whole[:, 2 * width].astype(jnp.int32) * 32 + whole[:, 2 * width + 1].astype(jnp.int32)
    grouped = query.reshape(rows, KVH, group, HD)
    scores = jnp.einsum("rgjd,sgd->gjrs", grouped, keys, preferred_element_type=jnp.float32) * (
        1.0 / math.sqrt(HD)
    )
    allowed = key_pos[None, :] <= positions[:, None]
    scores = jnp.where(allowed[None, None], scores, NEG_FILL)
    sink = sinks.reshape(KVH, group)[:, :, None]
    top = jnp.maximum(jnp.max(scores, axis=-1), sink)
    weights = jnp.exp(scores - top[..., None])
    total = jnp.sum(weights, axis=-1) + jnp.exp(sink - top)
    accum = jnp.einsum(
        "gjrs,sgd->gjrd",
        weights.astype(jnp.bfloat16),
        values,
        preferred_element_type=jnp.float32,
    )
    attended = accum / total[..., None]
    return jnp.transpose(attended, (2, 0, 1, 3)).reshape(rows, QH * HD).astype(jnp.bfloat16)


def whole_projection(o_weight):
    chips = lax.axis_size("exp") // 2
    same_core = [[2 * chip + core for chip in range(chips)] for core in range(2)]
    mine = lax.all_gather(o_weight, "exp", axis=0, axis_index_groups=same_core)
    other = from_partner(mine, "exp", 0)
    return mine, other


def feed_forward(block, w_gate, w_up, w_down):
    flat = block.reshape(-1, D)
    gate = jnp.dot(flat, w_gate, preferred_element_type=jnp.float32)
    lifted = jnp.dot(flat, w_up, preferred_element_type=jnp.float32)
    active = (gate * jax.nn.sigmoid(1.702 * gate) * (lifted + 1.0)).astype(jnp.bfloat16)
    return jnp.dot(active, w_down, preferred_element_type=jnp.float32)


def body(
    query,
    key_value,
    positions,
    resid,
    sinks,
    o_weight,
    norm_gain,
    expert_ids,
    route_weights,
    w_gate,
    w_up,
    w_down,
):
    rows = query.shape[1]
    mine, other = whole_projection(o_weight)
    attended = attend(query[0], key_value[0], positions[0], sinks)
    chips = lax.axis_size("exp") // 2
    halves = attended.reshape(rows, chips, 2, -1)
    core = lax.axis_index("exp") % 2
    even, odd = halves[:, :, 0].reshape(rows, -1), halves[:, :, 1].reshape(rows, -1)
    projected = jnp.dot(
        jnp.where(core == 0, even, odd), mine.reshape(-1, D), preferred_element_type=jnp.float32
    ) + jnp.dot(
        jnp.where(core == 0, odd, even), other.reshape(-1, D), preferred_element_type=jnp.float32
    )
    mixed = resid[0].astype(jnp.float32) + projected
    normed = (
        mixed * lax.rsqrt(jnp.mean(mixed * mixed, axis=-1, keepdims=True) + 1e-05) * norm_gain
    ).astype(jnp.bfloat16)
    n_ctx = lax.axis_size("ctx")
    n_exp = lax.axis_size("exp")
    n_experts = n_ctx * n_exp // SLICES
    per_row = n_exp // SLICES
    cap = max(2, rows * TOP // n_experts)
    n_slots = n_experts * cap
    chosen = expert_ids[0].reshape(rows * TOP)
    onehot = chosen[:, None] == jnp.arange(n_experts, dtype=jnp.int32)[None, :]
    order = jnp.arange(rows * TOP, dtype=jnp.int32)
    earlier = (order[None, :] < order[:, None]).astype(jnp.bfloat16)
    before = jnp.dot(earlier, onehot.astype(jnp.bfloat16), preferred_element_type=jnp.float32)
    rank = jnp.sum(jnp.where(onehot, before, 0.0), axis=1).astype(jnp.int32)
    slot = (chosen % per_row * n_ctx + chosen // per_row) * cap + rank
    placed = slot.reshape(rows, TOP)[:, :, None] == jnp.arange(n_slots, dtype=jnp.int32)
    taken = jnp.any(placed, axis=1).astype(jnp.bfloat16)
    combine = jnp.sum(jnp.where(placed, route_weights[0][:, :, None], 0.0), axis=1)
    outgoing = (
        lax.dot_general(
            taken, normed, (((0,), (0,)), ((), ())), preferred_element_type=jnp.float32
        )
        .astype(jnp.bfloat16)
        .reshape(per_row, n_ctx, cap, D)
    )
    arrived = lax.all_to_all(outgoing, "ctx", split_axis=1, concat_axis=1, tiled=True)
    pieces = arrived.reshape(n_exp, n_ctx // SLICES, cap, D)
    held = lax.all_to_all(pieces, "exp", split_axis=0, concat_axis=0, tiled=True)
    ffn = lambda block: feed_forward(block, w_gate, w_up, w_down)
    near = held.reshape(-1, D)
    near_core = from_partner(near, "exp", 0)
    far = from_partner(near, "exp", 1)
    far_core = from_partner(far, "exp", 0)
    out_near = ffn(near)
    back_near = from_partner(ffn(near_core).astype(jnp.bfloat16), "exp", 0)
    back_far = from_partner(ffn(far_core).astype(jnp.bfloat16), "exp", 0)
    sum_far = (ffn(far) + back_far.astype(jnp.float32)).astype(jnp.bfloat16)
    returned_far = from_partner(sum_far, "exp", 1)
    result = out_near + back_near.astype(jnp.float32) + returned_far.astype(jnp.float32)
    back = lax.all_to_all(
        result.astype(jnp.bfloat16).reshape(held.shape),
        "exp",
        split_axis=0,
        concat_axis=0,
        tiled=True,
    )
    returned = lax.all_to_all(
        back.reshape(per_row, n_ctx, cap, D), "ctx", split_axis=1, concat_axis=1, tiled=True
    )
    gathered = jnp.dot(
        combine,
        returned.reshape(n_slots, D).astype(jnp.float32),
        precision=lax.Precision.HIGHEST,
    )
    final = mixed + gathered
    return final.astype(jnp.bfloat16)[None]


def solution(mesh):
    return jax.shard_map(
        body,
        mesh=mesh,
        in_specs=(
            P("exp", "ctx", None),
            P("exp", "ctx", None, None),
            P("exp", "ctx"),
            P("exp", "ctx", None),
            P(),
            P("exp", None),
            P(),
            P("exp", "ctx", None),
            P("exp", "ctx", None),
            P(None, ("ctx", "exp")),
            P(None, ("ctx", "exp")),
            P(("ctx", "exp"), None),
        ),
        out_specs=P("exp", "ctx", None),
        check_vma=False,
    )
```

time: 282 us -> 252 us (0.89)
  blocking collectives: 114 us -> 61.5 us
  waiting for transfers between devices: 86.3 us -> 115 us
  matrix products: 22 us -> 30.9 us
  local copies, waits for them, and re-layouts: 21.9 us -> 15.4 us
  other arithmetic: 9.81 us -> 4.72 us
  starting transfers between devices: 13.6 us -> 9.42 us
    all_to_all x1, blocking collectives: 75.1 us -> 23.9 us  [body(): lax.all_to_all(result.astype(jnp.bfloat16).reshape(held.shape), 'exp', sp...]
    all_gather x1, waiting for transfers between devices: 26.5 us -> 64.6 us  [whole_projection(): mine = lax.all_gather(o_weight, 'exp', axis=0, axis_index_groups=same_core)]
    dot_general x11 -> x15, matrix products: 22 us -> 30.9 us  [the longest x4 16.2 us: feed_forward(): return jnp.dot(active, w_down, preferred_element_type=jnp.float32)]
    all_gather x0 -> x1, local copies, waits for them, and re-layouts: none -> 6.4 us  [whole_projection(): mine = lax.all_gather(o_weight, 'exp', axis=0, axis_index_groups=same_core)]
    convert_element_type x4 -> x6, local copies, waits for them, and re-layouts: 7.1 us -> 1.43 us  [the longest x2 0.71 us: attend(): jnp.transpose(attended, (2, 0, 1, 3)).reshape(rows, QH * HD)]
    ppermute x6 -> x3, starting transfers between devices: 10 us -> 4.49 us  [passed_along(): lax.ppermute(value, axis, [(i, (i + by) % length) for i in range(length)])]
    ppermute x6 -> x3, waiting for transfers between devices: 10.4 us -> 5.26 us  [passed_along(): lax.ppermute(value, axis, [(i, (i + by) % length) for i in range(length)])]
    ppermute x2 -> x7, waiting for transfers between devices: 38.1 us -> 34 us  [from_partner(): return lax.ppermute(block, axis, route)]
  transfers between devices with their start and end apart: 10 -> 12, of which waited for: 10 -> 8; matrix products, arithmetic and copies ran while one was open for 7% -> 13% of each run, Pallas kernels for 0% -> 0%
where the time goes in v1:
time: 252 us; the launch traced here: 251 us
  waiting for transfers between devices  115 us (46%)
  blocking collectives  61.5 us (24%)
  matrix products  30.9 us (12%)
  local copies, waits for them, and re-layouts  15.4 us (6%)
  between operations  13.7 us (5%)
  starting transfers between devices  9.42 us (4%)
  other arithmetic  4.72 us (2%)
    all_gather x1, waiting for transfers between devices, whole_projection(): mine = lax.all_gather(o_weight, 'exp', axis=0, axis_index_groups=same_core)  64.6 us
    ppermute x7, waiting for transfers between devices, from_partner(): return lax.ppermute(block, axis, route)  34 us
    all_to_all x1, blocking collectives, body(): lax.all_to_all(result.astype(jnp.bfloat16).reshape(held.shape), 'exp', sp...  23.9 us
    all_to_all x1, blocking collectives, body(): lax.all_to_all(pieces, 'exp', split_axis=0, concat_axis=0, tiled=True)  23.4 us
    dot_general x4, matrix products, feed_forward(): return jnp.dot(active, w_down, preferred_element_type=jnp.float32)  16.2 us
    all_to_all x1, blocking collectives, body(): lax.all_to_all(outgoing, 'ctx', split_axis=1, concat_axis=1, tiled=True)  14.2 us
    all_to_all x1, waiting for transfers between devices, body(): lax.all_to_all(back.reshape(per_row, n_ctx, cap, D), 'ctx', split_axis=1,...  10.6 us
    dot_general x4, matrix products, feed_forward(): gate = jnp.dot(flat, w_gate, preferred_element_type=jnp.float32)  7.56 us
  transfers between devices with their start and end apart: 12, of which 8 were waited for; matrix products, arithmetic and copies ran while one was open for 13% of the time, Pallas kernels for 0%

profile of v1, /device:TPU:0, one launch (start us, length us, event | category | flops | bytes accessed | tf_op | source)
XLA Modules:
  0.0 250.8 jit_solution(4089411752574779633)
XLA Ops:
  6.5 0.7 all-gather.3.cloned.1.call-update
  7.3 64.6 %all-gather.3.cloned.1.call-done = bf16[1024,1440]{0,1:T(8,128)(2,1)} async-done(((bf16[256,1440]{0,1:T(8,128)(2,1)}), bf16[1024,1440]{0,1:T(8,128)(2,1)}) %all-gather.3.cloned.1.call-update) | async-done | bytes 2949136 | tf_op jit(solution)/shard_map/all_gather | solution.py:79
  71.9 6.4 %reshape.282 = bf16[4,256,1440]{1,0,2:T(4,128)(2,1)} reshape(bf16[1024,1440]{0,1:T(8,128)(2,1)} %all-gather.3.cloned.1.call-done) | data formatting | bytes 5898240 | tf_op jit(solution)/shard_map/all_gather | solution.py:79
  78.5 1.6 collective-permute-start
  80.1 1.5 collective-permute-start.1
  81.5 1.5 collective-permute-start.2
  83.0 0.5 reshape_squeeze.12
  83.8 0.2 fusion.10
  84.4 2.1 collective-permute-done
  86.5 3.1 %collective-permute-done.1 = bf16[64,640]{0,1:T(8,128)(2,1)S(1)} collective-permute-done((bf16[64,640]{0,1:T(8,128)(2,1)S(1)}, bf16[64,640]{0,1:T(8,128)(2,1)S(1)}, u32[]{:S(2)}, u32[]{:S(2)}) %collective-permute-start.1) | collective-permute-done | bytes 81952 | tf_op jit(solution)/shard_map/ppermute | solution.py:21
  89.7 0.2 pad_maximum_fusion.7
  90.0 0.6 fusion.54
  90.6 0.7 fusion.3
  91.4 0.8 fusion.6
  92.2 0.3 copy.73
  92.5 0.4 convert_element_type.116
  92.9 1.2 fusion.21
  94.2 2.8 %fusion.55 = f32[64,1440]{1,0:T(8,128)S(1)} fusion(bf16[64,1024]{1,0:T(8,128)(2,1)S(1)} %bitcast.129, bf16[1024,1440]{0,1:T(8,128)(2,1)} %all-gather.3.cloned.1.call-done), kind=kOutput, calls=%fused_computation.107 | convolution fusion | flops 188743680 | bytes 3448832 | tf_op jit(solution)/shard_map/dot_general | solution.py:113
  97.1 2.6 %copy.91 = bf16[180,8,4,256]{3,1,2,0:T(8,128)(2,1)S(1)} copy(bf16[180,8,4,256]{3,2,1,0:T(4,128)(2,1)} %bitcast.39) | data formatting | bytes 5898240
  99.7 1.1 multiply_reduce_fusion
  100.8 0.5 convolution_convert_fusion.2
  101.3 0.3 copy.76
  101.6 14.2 %all_to_all.20 = bf16[2,4,32,1440]{3,2,0,1:T(8,128)(2,1)S(1)} all-to-all(bf16[2,4,32,1440]{3,2,0,1:T(8,128)(2,1)S(1)} %copy.77), channel_id=1, replica_groups=mesh['ctx'=4,'exp'=8] {'ctx'}, dimensions={1} | all-to-all | bytes 1474560 | tf_op jit(solution)/shard_map/all_to_all | solution.py:145
  115.9 23.4 %all_to_all.21 = bf16[8,1,32,1440]{3,2,1,0:T(8,128)(2,1)S(1)} all-to-all(bf16[8,1,32,1440]{3,2,1,0:T(8,128)(2,1)S(1)} %bitcast.118), channel_id=1, replica_groups=mesh['ctx'=4,'exp'=8] {'exp'}, dimensions={0} | all-to-all | bytes 1474560 | tf_op jit(solution)/shard_map/all_to_all | solution.py:147
  139.3 1.1 copy.80
  140.4 18.1 %collective-permute-done.6 = bf16[256,1440]{0,1:T(8,128)(2,1)S(1)} collective-permute-done((bf16[256,1440]{0,1:T(8,128)(2,1)}, bf16[256,1440]{0,1:T(8,128)(2,1)S(1)}, u32[]{:S(2)}, u32[]{:S(2)}) %collective-permute-start.6) | collective-permute-done | bytes 737312 | tf_op jit(solution)/shard_map/ppermute | solution.py:31
  158.5 0.9 copy-done.2
  159.4 0.5 collective-permute-start.4
  159.9 2.7 %collective-permute-done.7 = bf16[256,1440]{0,1:T(8,128)(2,1)S(1)} collective-permute-done((bf16[256,1440]{0,1:T(8,128)(2,1)S(1)}, bf16[256,1440]{0,1:T(8,128)(2,1)S(1)}, u32[]{:S(2)}, u32[]{:S(2)}) %collective-permute-start.7) | collective-permute-done | bytes 737312 | tf_op jit(solution)/shard_map/ppermute | solution.py:31
  162.6 0.9 copy-done.3
  163.5 1.3 fusion.59
  164.8 4.0 %convolution_convert_fusion = bf16[256,1440]{0,1:T(8,128)(2,1)} fusion(bf16[360,1440]{1,0:T(8,128)(2,1)S(1)} %copy-done, f32[256,360]{0,1:T(8,128)} %fusion.59, bf16[256,1440]{0,1:T(8,128)(2,1)} %copy-done.3, bf16[1440,360]{1,0:T(8,128)(2,1)} %param.22), kind=kOutput, calls=%fused_computation | convolution fusion | flops 531947520 | bytes 3916800 | tf_op jit(solution)/shard_map/dot_general | solution.py:89
  168.9 2.5 fusion.57
  171.4 4.0 %convolution_convert_fusion.1 = bf16[256,1440]{0,1:T(8,128)(2,1)} fusion(bf16[360,1440]{1,0:T(8,128)(2,1)S(1)} %copy-done, f32[256,360]{0,1:T(8,128)} %fusion.57, bf16[256,1440]{0,1:T(8,128)(2,1)} %collective-permute-done.4, bf16[1440,360]{1,0:T(8,128)(2,1)} %param.22), kind=kOutput, calls=%fused_computation.1 | convolution fusion | flops 531947520 | bytes 3916800 | tf_op jit(solution)/shard_map/dot_general | solution.py:89
  175.4 0.4 collective-permute-start.5
  175.7 2.4 fusion.58
  178.2 4.2 %add_convert_fusion.1 = bf16[256,1440]{0,1:T(8,128)(2,1)} fusion(bf16[256,1440]{0,1:T(8,128)(2,1)} %collective-permute-done.8, bf16[360,1440]{1,0:T(8,128)(2,1)S(1)} %copy-done, f32[256,360]{0,1:T(8,128)} %fusion.58, bf16[256,1440]{0,1:T(8,128)(2,1)} %copy-done.2, bf16[1440,360]{1,0:T(8,128)(2,1)} %param.22), kind=kOutput, calls=%fused_computation.13 | convolution fusion | flops 532684800 | bytes 4654080 | tf_op jit(solution)/shard_map/dot_general | solution.py:89
  182.4 0.3 collective-permute-start.9
  182.7 1.3 fusion.56
  184.0 4.0 %fusion.9 = f32[256,1440]{0,1:T(8,128)} fusion(bf16[360,1440]{1,0:T(8,128)(2,1)S(1)} %copy-done, bf16[256,1440]{1,0:T(8,128)(2,1)S(1)} %bitcast.116, bf16[1440,360]{1,0:T(8,128)(2,1)} %param.22, f32[256,360]{0,1:T(8,128)} %fusion.56), kind=kOutput, calls=%fused_computation.23 | convolution fusion | flops 531578880 | bytes 4654080 | tf_op jit(solution)/shard_map/dot_general | solution.py:89
  188.0 13.2 %collective-permute-done.9 = bf16[256,1440]{0,1:T(8,128)(2,1)} collective-permute-done((bf16[256,1440]{0,1:T(8,128)(2,1)}, bf16[256,1440]{0,1:T(8,128)(2,1)}, u32[]{:S(2)}, u32[]{:S(2)}) %collective-permute-start.9) | collective-permute-done | bytes 737312 | tf_op jit(solution)/shard_map/ppermute | solution.py:31
  201.2 2.0 add_convert_fusion
  203.2 0.3 copy.82
  203.5 23.9 %all_to_all.22 = bf16[8,1,32,1440]{3,2,1,0:T(8,128)(2,1)S(1)} all-to-all(bf16[8,1,32,1440]{3,2,1,0:T(8,128)(2,1)S(1)} %bitcast.119), channel_id=1, replica_groups=mesh['ctx'=4,'exp'=8] {'exp'}, dimensions={0} | all-to-all | bytes 1474560 | tf_op jit(solution)/shard_map/all_to_all | solution.py:159
  227.4 0.9 copy.84
  228.4 3.6 %all-to-all-start.3 = ((bf16[2,4,32,1440]{3,2,0,1:T(8,128)(2,1)}), bf16[2,4,32,1440]{3,2,0,1:T(8,128)(2,1)S(1)}, u32[]{:S(2)}, u32[]{:S(2)}) async-start(bf16[2,4,32,1440]{3,2,0,1:T(8,128)(2,1)} %copy.84), calls=%async_computation.3 | async-start | bytes 1572864 | tf_op jit(solution)/shard_map/all_to_all | solution.py:166
  232.1 10.6 %all-to-all-done.3 = bf16[2,4,32,1440]{3,2,0,1:T(8,128)(2,1)S(1)} async-done(((bf16[2,4,32,1440]{3,2,0,1:T(8,128)(2,1)}), bf16[2,4,32,1440]{3,2,0,1:T(8,128)(2,1)S(1)}, u32[]{:S(2)}, u32[]{:S(2)}) %all-to-all-start.3) | async-done | bytes 737312 | tf_op jit(solution)/shard_map/all_to_all | solution.py:166
  242.8 1.2 fusion.2
  (55 shorter events, 1.7 us)
Async XLA Ops:
  6.5 158.3 %copy-start = (bf16[360,1440]{1,0:T(8,128)(2,1)S(1)}, bf16[360,1440]{1,0:T(8,128)(2,1)}, u32[]{:S(2)}) copy-start(bf16[360,1440]{1,0:T(8,128)(2,1)} %param.23) | copy-start | bytes 3110404
  6.5 65.3 %all-gather.3.cloned.1.call-start = ((), (), s32[]{:S(2)}) async-start(), calls=%async_computation.4 | async-start | bytes 3686400 | tf_op jit(solution)/shard_map/all_gather | solution.py:79
  7.3 71.0 %copy-start.11 = (s32[1,64]{1,0:T(1,128)S(1)}, s32[1,64]{1,0:T(1,128)}, u32[]{:S(2)}) copy-start(s32[1,64]{1,0:T(1,128)} %param.14) | copy-start | bytes 772
  7.3 71.0 %copy-start.6 = (bf16[1,64,2,256]{3,2,1,0:T(2,128)(2,1)S(1)}, bf16[1,64,2,256]{3,2,1,0:T(2,128)(2,1)}, u32[]{:S(2)}) copy-start(bf16[1,64,2,256]{3,2,1,0:T(2,128)(2,1)} %param.13) | copy-start | bytes 196612
  7.3 75.7 %copy-start.4 = (bf16[1,64,2048]{2,1,0:T(8,128)(2,1)S(1)}, bf16[1,64,2048]{2,1,0:T(8,128)(2,1)}, u32[]{:S(2)}) copy-start(bf16[1,64,2048]{2,1,0:T(8,128)(2,1)} %param.12) | copy-start | bytes 786436
  78.3 5.3 %copy-start.10 = (f32[32]{0:T(128)S(1)}, f32[32]{0:T(128)}, u32[]{:S(2)}) copy-start(f32[32]{0:T(128)} %param.16) | copy-start | bytes 388
  78.3 5.4 %copy-start.8 = (s32[1,64,4]{1,2,0:T(4,128)S(1)}, s32[1,64,4]{1,2,0:T(4,128)}, u32[]{:S(2)}) copy-start(s32[1,64,4]{1,2,0:T(4,128)} %param.19) | copy-start | bytes 3076
  78.3 18.8 %collective-permute-start.3 = (bf16[4,256,1440]{1,0,2:T(4,128)(2,1)}, bf16[4,256,1440]{1,0,2:T(4,128)(2,1)}, u32[]{:S(2)}, u32[]{:S(2)}) collective-permute-start(bf16[4,256,1440]{1,0,2:T(4,128)(2,1)} %reshape.282), channel_id=1, source_target_pairs={{0,1},{1,0},{2,3},{3,2},{4,5},{5,4},{6,7},{7,6},{8,9},{9,8},{10,11... | collective-permute-start | bytes 8847368 | tf_op jit(solution)/shard_map/ppermute | solution.py:31
  78.5 8.0 %collective-permute-start = (bf16[64,640]{0,1:T(8,128)(2,1)S(1)}, bf16[64,640]{0,1:T(8,128)(2,1)S(1)}, u32[]{:S(2)}, u32[]{:S(2)}) collective-permute-start(bf16[64,640]{0,1:T(8,128)(2,1)S(1)} %pad_maximum_fusion), channel_id=1, source_target_pairs={{0,8},{8,16},{16,24},{24,0},{1,9},{9,17},{17,25},{25,1},{2,10},{10... | collective-permute-start | bytes 245768 | tf_op jit(solution)/shard_map/ppermute | solution.py:21
  80.1 9.5 %collective-permute-start.1 = (bf16[64,640]{0,1:T(8,128)(2,1)S(1)}, bf16[64,640]{0,1:T(8,128)(2,1)S(1)}, u32[]{:S(2)}, u32[]{:S(2)}) collective-permute-start(bf16[64,640]{0,1:T(8,128)(2,1)S(1)} %pad_maximum_fusion), channel_id=1, source_target_pairs={{0,16},{8,24},{16,0},{24,8},{1,17},{9,25},{17,1},{25,9},{2,18},{10... | collective-permute-start | bytes 245768 | tf_op jit(solution)/shard_map/ppermute | solution.py:21
  81.5 8.1 %collective-permute-start.2 = (bf16[64,640]{0,1:T(8,128)(2,1)S(1)}, bf16[64,640]{0,1:T(8,128)(2,1)S(1)}, u32[]{:S(2)}, u32[]{:S(2)}) collective-permute-start(bf16[64,640]{0,1:T(8,128)(2,1)S(1)} %pad_maximum_fusion), channel_id=1, source_target_pairs={{0,24},{8,0},{16,8},{24,16},{1,25},{9,1},{17,9},{25,17},{2,26},{10... | collective-permute-start | bytes 245768 | tf_op jit(solution)/shard_map/ppermute | solution.py:21
  97.0 2.6 %copy-start.5 = (bf16[1,64,1440]{2,1,0:T(8,128)(2,1)S(1)}, bf16[1,64,1440]{2,1,0:T(8,128)(2,1)}, u32[]{:S(2)}) copy-start(bf16[1,64,1440]{2,1,0:T(8,128)(2,1)} %param.15) | copy-start | bytes 552964
  99.7 1.1 copy-start.7
  139.3 24.2 %copy-start.1 = (bf16[1440,360]{1,0:T(8,128)(2,1)S(1)}, bf16[1440,360]{1,0:T(8,128)(2,1)}, u32[]{:S(2)}) copy-start(bf16[1440,360]{1,0:T(8,128)(2,1)} %param.21) | copy-start | bytes 3110404
  140.4 18.1 %collective-permute-start.6 = (bf16[256,1440]{0,1:T(8,128)(2,1)}, bf16[256,1440]{0,1:T(8,128)(2,1)S(1)}, u32[]{:S(2)}, u32[]{:S(2)}) collective-permute-start(bf16[256,1440]{0,1:T(8,128)(2,1)} %copy.80), channel_id=1, source_target_pairs={{0,2},{2,0},{1,3},{3,1},{4,6},{6,4},{5,7},{7,5},{8,10},{10,8},{9,1... | collective-permute-start | bytes 2211848 | tf_op jit(solution)/shard_map/ppermute | solution.py:31
  158.5 0.9 copy-start.2
  159.4 3.2 %collective-permute-start.7 = (bf16[256,1440]{0,1:T(8,128)(2,1)S(1)}, bf16[256,1440]{0,1:T(8,128)(2,1)S(1)}, u32[]{:S(2)}, u32[]{:S(2)}) collective-permute-start(bf16[256,1440]{0,1:T(8,128)(2,1)S(1)} %collective-permute-done.6), channel_id=1, source_target_pairs={{0,1},{1,0},{2,3},{3,2},{4,5},{5,4},{6,7},{7,6},{8,9},{9,8},{10,11... | collective-permute-start | bytes 2211848 | tf_op jit(solution)/shard_map/ppermute | solution.py:31
  159.4 9.6 %collective-permute-start.4 = (bf16[256,1440]{0,1:T(8,128)(2,1)}, bf16[256,1440]{0,1:T(8,128)(2,1)}, u32[]{:S(2)}, u32[]{:S(2)}) collective-permute-start(bf16[256,1440]{0,1:T(8,128)(2,1)} %copy.80), channel_id=1, source_target_pairs={{0,1},{1,0},{2,3},{3,2},{4,5},{5,4},{6,7},{7,6},{8,9},{9,8},{10,11... | collective-permute-start | bytes 2211848 | tf_op jit(solution)/shard_map/ppermute | solution.py:31
  162.6 0.9 copy-start.3
  168.8 9.4 %collective-permute-start.8 = (bf16[256,1440]{0,1:T(8,128)(2,1)}, bf16[256,1440]{0,1:T(8,128)(2,1)}, u32[]{:S(2)}, u32[]{:S(2)}) collective-permute-start(bf16[256,1440]{0,1:T(8,128)(2,1)} %convolution_convert_fusion), channel_id=1, source_target_pairs={{0,1},{1,0},{2,3},{3,2},{4,5},{5,4},{6,7},{7,6},{8,9},{9,8},{10,11... | collective-permute-start | bytes 2211848 | tf_op jit(solution)/shard_map/ppermute | solution.py:31
  175.4 12.7 %collective-permute-start.5 = (bf16[256,1440]{0,1:T(8,128)(2,1)}, bf16[256,1440]{0,1:T(8,128)(2,1)}, u32[]{:S(2)}, u32[]{:S(2)}) collective-permute-start(bf16[256,1440]{0,1:T(8,128)(2,1)} %convolution_convert_fusion.1), channel_id=1, source_target_pairs={{0,1},{1,0},{2,3},{3,2},{4,5},{5,4},{6,7},{7,6},{8,9},{9,8},{10,11... | collective-permute-start | bytes 2211848 | tf_op jit(solution)/shard_map/ppermute | solution.py:31
  182.4 18.8 %collective-permute-start.9 = (bf16[256,1440]{0,1:T(8,128)(2,1)}, bf16[256,1440]{0,1:T(8,128)(2,1)}, u32[]{:S(2)}, u32[]{:S(2)}) collective-permute-start(bf16[256,1440]{0,1:T(8,128)(2,1)} %add_convert_fusion.1), channel_id=1, source_target_pairs={{0,2},{2,0},{1,3},{3,1},{4,6},{6,4},{5,7},{7,5},{8,10},{10,8},{9,1... | collective-permute-start | bytes 2211848 | tf_op jit(solution)/shard_map/ppermute | solution.py:31
  228.4 3.6 %copy-start.9 = (f32[1,64,4]{1,2,0:T(4,128)S(1)}, f32[1,64,4]{1,2,0:T(4,128)}, u32[]{:S(2)}) copy-start(f32[1,64,4]{1,2,0:T(4,128)} %param.20) | copy-start | bytes 3076
  228.4 14.3 %all-to-all-start.3 = ((bf16[2,4,32,1440]{3,2,0,1:T(8,128)(2,1)}), bf16[2,4,32,1440]{3,2,0,1:T(8,128)(2,1)S(1)}, u32[]{:S(2)}, u32[]{:S(2)}) async-start(bf16[2,4,32,1440]{3,2,0,1:T(8,128)(2,1)} %copy.84), calls=%async_computation.3 | async-start | bytes 1572864 | tf_op jit(solution)/shard_map/all_to_all | solution.py:166
Sparse Core Ops, SparseCore 0:
  8.9 62.8 all-gather.2

commit v2 on v1

--- a/solution.py
+++ b/solution.py
@@ -73,12 +73,23 @@
     return jnp.transpose(attended, (2, 0, 1, 3)).reshape(rows, QH * HD).astype(jnp.bfloat16)
 
 
-def whole_projection(o_weight):
+def to_next_chip(block, by):
+    count = lax.axis_size("exp")
+    route = [(i, i + 2 * by) for i in range(count) if 0 <= i + 2 * by < count]
+    return lax.ppermute(block, "exp", route)
+
+
+def projection_blocks(o_weight):
     chips = lax.axis_size("exp") // 2
-    same_core = [[2 * chip + core for chip in range(chips)] for core in range(2)]
-    mine = lax.all_gather(o_weight, "exp", axis=0, axis_index_groups=same_core)
-    other = from_partner(mine, "exp", 0)
-    return mine, other
+    chip = lax.axis_index("exp") // 2
+    upward, downward = [o_weight], [o_weight]
+    for _ in range(1, chips):
+        upward.append(to_next_chip(upward[-1], 1))
+        downward.append(to_next_chip(downward[-1], -1))
+    blocks = [o_weight]
+    for back in range(1, chips):
+        blocks.append(jnp.where(back <= chip, upward[back], downward[chips - back]))
+    return blocks, [from_partner(block, "exp", 0) for block in blocks]
 
 
 def feed_forward(block, w_gate, w_up, w_down):
@@ -104,17 +115,19 @@
     w_down,
 ):
     rows = query.shape[1]
-    mine, other = whole_projection(o_weight)
+    blocks, partner_blocks = projection_blocks(o_weight)
     attended = attend(query[0], key_value[0], positions[0], sinks)
     chips = lax.axis_size("exp") // 2
     halves = attended.reshape(rows, chips, 2, -1)
-    core = lax.axis_index("exp") % 2
-    even, odd = halves[:, :, 0].reshape(rows, -1), halves[:, :, 1].reshape(rows, -1)
-    projected = jnp.dot(
-        jnp.where(core == 0, even, odd), mine.reshape(-1, D), preferred_element_type=jnp.float32
-    ) + jnp.dot(
-        jnp.where(core == 0, odd, even), other.reshape(-1, D), preferred_element_type=jnp.float32
-    )
+    chip, core = lax.axis_index("exp") // 2, lax.axis_index("exp") % 2
+    even, odd = halves[:, :, 0], halves[:, :, 1]
+    here, there = jnp.where(core == 0, even, odd), jnp.where(core == 0, odd, even)
+    projected = jnp.zeros((rows, D), jnp.float32)
+    for back in range(chips):
+        source = (chip - back + chips) % chips
+        for side, block in ((here, blocks[back]), (there, partner_blocks[back])):
+            columns = lax.dynamic_index_in_dim(side, source, 1, keepdims=False)
+            projected += jnp.dot(columns, block, preferred_element_type=jnp.float32)
     mixed = resid[0].astype(jnp.float32) + projected
     normed = (
         mixed * lax.rsqrt(jnp.mean(mixed * mixed, axis=-1, keepdims=True) + 1e-05) * norm_gain

time: 252 us -> 222 us (0.88)
  waiting for transfers between devices: 115 us -> 79.5 us
  starting transfers between devices: 9.42 us -> 28.2 us
  between operations: 13.7 us -> 0.55 us
  local copies, waits for them, and re-layouts: 15.4 us -> 8.07 us
  other arithmetic: 4.72 us -> 8.62 us
  blocking collectives: 61.5 us -> 65.3 us
    all_gather x1 -> x0, waiting for transfers between devices: 64.6 us -> none  [whole_projection(): mine = lax.all_gather(o_weight, 'exp', axis=0, axis_index_groups=same_core)]
    ppermute x0 -> x6, waiting for transfers between devices: none -> 33.9 us  [to_next_chip(): return lax.ppermute(block, 'exp', route)]
    ppermute x0 -> x6, starting transfers between devices: none -> 17.2 us  [to_next_chip(): return lax.ppermute(block, 'exp', route)]
    all_gather x1 -> x0, local copies, waits for them, and re-layouts: 6.4 us -> none  [whole_projection(): mine = lax.all_gather(o_weight, 'exp', axis=0, axis_index_groups=same_core)]
    ppermute x3, waiting for transfers between devices: 5.26 us -> 0.01 us  [passed_along(): lax.ppermute(value, axis, [(i, (i + by) % length) for i in range(length)])]
    all_to_all x1, blocking collectives: 23.4 us -> 27.1 us  [body(): lax.all_to_all(pieces, 'exp', split_axis=0, concat_axis=0, tiled=True)]
    unnamed x28 -> x21, local copies, waits for them, and re-layouts: 4.5 us -> 1.2 us
    ppermute x7 -> x10, waiting for transfers between devices: 34 us -> 35.1 us  [from_partner(): return lax.ppermute(block, axis, route)]
  transfers between devices with their start and end apart: 12 -> 20, of which waited for: 8 -> 11; matrix products, arithmetic and copies ran while one was open for 13% -> 17% of each run, Pallas kernels for 0% -> 0%
where the time goes in v2:
time: 222 us; the launch traced here: 221 us
  waiting for transfers between devices  79.5 us (36%)
  blocking collectives  65.3 us (29%)
  matrix products  31 us (14%)
  starting transfers between devices  28.2 us (13%)
  other arithmetic  8.62 us (4%)
  local copies, waits for them, and re-layouts  8.07 us (4%)
    ppermute x10, waiting for transfers between devices, from_partner(): return lax.ppermute(block, axis, route)  35.1 us
    ppermute x6, waiting for transfers between devices, to_next_chip(): return lax.ppermute(block, 'exp', route)  33.9 us
    all_to_all x1, blocking collectives, body(): lax.all_to_all(pieces, 'exp', split_axis=0, concat_axis=0, tiled=True)  27.1 us
    all_to_all x1, blocking collectives, body(): lax.all_to_all(result.astype(jnp.bfloat16).reshape(held.shape), 'exp', sp...  23.9 us
    ppermute x6, starting transfers between devices, to_next_chip(): return lax.ppermute(block, 'exp', route)  17.2 us
    dot_general x4, matrix products, feed_forward(): return jnp.dot(active, w_down, preferred_element_type=jnp.float32)  16.1 us
    all_to_all x1, blocking collectives, body(): lax.all_to_all(outgoing, 'ctx', split_axis=1, concat_axis=1, tiled=True)  14.3 us
    all_to_all x1, waiting for transfers between devices, body(): lax.all_to_all(back.reshape(per_row, n_ctx, cap, D), 'ctx', split_axis=1,...  10.6 us
  transfers between devices with their start and end apart: 20, of which 11 were waited for; matrix products, arithmetic and copies ran while one was open for 17% of the time, Pallas kernels for 0%

profile of v2, /device:TPU:0, one launch (start us, length us, event | category | flops | bytes accessed | tf_op | source)
XLA Modules:
  0.0 221.2 jit_solution(1443394524258406054)
XLA Ops:
  0.0 0.8 fusion.66
  0.8 1.0 copy.88
  1.8 0.7 pad_maximum_fusion
  2.5 2.9 %collective-permute-start = (bf16[64,640]{0,1:T(8,128)(2,1)}, bf16[64,640]{0,1:T(8,128)(2,1)S(1)}, u32[]{:S(2)}, u32[]{:S(2)}) collective-permute-start(bf16[64,640]{0,1:T(8,128)(2,1)} %pad_maximum_fusion), channel_id=1, source_target_pairs={{0,8},{8,16},{16,24},{24,0},{1,9},{9,17},{17,25},{25,1},{2,10},{10... | collective-permute-start | bytes 245768 | tf_op jit(solution)/shard_map/ppermute | solution.py:21
  5.4 1.5 collective-permute-start.1
  6.9 1.4 collective-permute-start.2
  8.4 1.3 collective-permute-start.5
  9.8 1.5 reshape_squeeze.10
  12.1 4.6 %collective-permute-start.4 = (bf16[256,1440]{0,1:T(8,128)(2,1)}, bf16[256,1440]{0,1:T(8,128)(2,1)S(1)}, u32[]{:S(2)}, u32[]{:S(2)}) collective-permute-start(bf16[256,1440]{0,1:T(8,128)(2,1)} %param.17), channel_id=1, source_target_pairs={{0,2},{1,3},{2,4},{3,5},{4,6},{5,7},{8,10},{9,11},{10,12},{11,13},... | collective-permute-start | bytes 2211848 | tf_op jit(solution)/shard_map/ppermute | solution.py:79
  16.7 0.8 fusion.63
  17.7 1.1 pad_maximum_fusion.7
  19.4 0.7 fusion.6
  20.2 9.2 %collective-permute-done.5 = bf16[256,1440]{0,1:T(8,128)(2,1)S(1)} collective-permute-done((bf16[256,1440]{0,1:T(8,128)(2,1)}, bf16[256,1440]{0,1:T(8,128)(2,1)S(1)}, u32[]{:S(2)}, u32[]{:S(2)}) %collective-permute-start.5) | collective-permute-done | bytes 737312 | tf_op jit(solution)/shard_map/ppermute | solution.py:79
  29.4 1.3 collective-permute-start.6
  30.7 0.8 fusion.9
  32.2 0.9 collective-permute-done.4
  33.1 4.3 %collective-permute-start.9 = (bf16[256,1440]{0,1:T(8,128)(2,1)S(1)}, bf16[256,1440]{0,1:T(8,128)(2,1)S(1)}, u32[]{:S(2)}, u32[]{:S(2)}) collective-permute-start(bf16[256,1440]{0,1:T(8,128)(2,1)S(1)} %collective-permute-done.4), channel_id=1, source_target_pairs={{0,2},{1,3},{2,4},{3,5},{4,6},{5,7},{8,10},{9,11},{10,12},{11,13},... | collective-permute-start | bytes 2211848 | tf_op jit(solution)/shard_map/ppermute | solution.py:79
  37.4 0.6 broadcast_select_fusion.4
  38.0 0.6 constant_dynamic-slice_fusion.1
  39.0 10.5 %collective-permute-done.6 = bf16[256,1440]{0,1:T(8,128)(2,1)} collective-permute-done((bf16[256,1440]{0,1:T(8,128)(2,1)S(1)}, bf16[256,1440]{0,1:T(8,128)(2,1)}, u32[]{:S(2)}, u32[]{:S(2)}) %collective-permute-start.6) | collective-permute-done | bytes 737312 | tf_op jit(solution)/shard_map/ppermute | solution.py:79
  49.5 1.3 collective-permute-start.7
  50.8 1.5 convolution_add_fusion.4
  52.7 4.4 %collective-permute-start.11 = (bf16[256,1440]{0,1:T(8,128)(2,1)S(1)}, bf16[256,1440]{0,1:T(8,128)(2,1)S(1)}, u32[]{:S(2)}, u32[]{:S(2)}) collective-permute-start(bf16[256,1440]{0,1:T(8,128)(2,1)S(1)} %collective-permute-done.9), channel_id=1, source_target_pairs={{0,2},{1,3},{2,4},{3,5},{4,6},{5,7},{8,10},{9,11},{10,12},{11,13},... | collective-permute-start | bytes 2211848 | tf_op jit(solution)/shard_map/ppermute | solution.py:79
  57.1 1.2 broadcast_select_fusion.1
  58.4 10.4 %collective-permute-done.7 = bf16[256,1440]{0,1:T(8,128)(2,1)S(1)} collective-permute-done((bf16[256,1440]{0,1:T(8,128)(2,1)}, bf16[256,1440]{0,1:T(8,128)(2,1)S(1)}, u32[]{:S(2)}, u32[]{:S(2)}) %collective-permute-start.7) | collective-permute-done | bytes 737312 | tf_op jit(solution)/shard_map/ppermute | solution.py:79
  69.0 2.5 %collective-permute-done.11 = bf16[256,1440]{0,1:T(8,128)(2,1)S(1)} collective-permute-done((bf16[256,1440]{0,1:T(8,128)(2,1)S(1)}, bf16[256,1440]{0,1:T(8,128)(2,1)S(1)}, u32[]{:S(2)}, u32[]{:S(2)}) %collective-permute-start.11) | collective-permute-done | bytes 737312 | tf_op jit(solution)/shard_map/ppermute | solution.py:79
  73.1 0.7 collective-permute-done.12
  75.7 14.3 %all_to_all.20 = bf16[2,4,32,1440]{3,2,0,1:T(8,128)(2,1)S(1)} all-to-all(bf16[2,4,32,1440]{3,2,0,1:T(8,128)(2,1)S(1)} %copy.77), channel_id=1, replica_groups=mesh['ctx'=4,'exp'=8] {'ctx'}, dimensions={1} | all-to-all | bytes 1474560 | tf_op jit(solution)/shard_map/all_to_all | solution.py:158
  90.1 27.1 %all_to_all.21 = bf16[8,1,32,1440]{3,2,1,0:T(8,128)(2,1)S(1)} all-to-all(bf16[8,1,32,1440]{3,2,1,0:T(8,128)(2,1)S(1)} %bitcast.137), channel_id=1, replica_groups=mesh['ctx'=4,'exp'=8] {'exp'}, dimensions={0} | all-to-all | bytes 1474560 | tf_op jit(solution)/shard_map/all_to_all | solution.py:160
  117.1 1.1 copy.80
  118.3 18.2 %collective-permute-done.15 = bf16[256,1440]{0,1:T(8,128)(2,1)} collective-permute-done((bf16[256,1440]{0,1:T(8,128)(2,1)}, bf16[256,1440]{0,1:T(8,128)(2,1)}, u32[]{:S(2)}, u32[]{:S(2)}) %collective-permute-start.15) | collective-permute-done | bytes 737312 | tf_op jit(solution)/shard_map/ppermute | solution.py:31
  136.9 2.9 %collective-permute-done.16 = bf16[256,1440]{0,1:T(8,128)(2,1)S(1)} collective-permute-done((bf16[256,1440]{0,1:T(8,128)(2,1)}, bf16[256,1440]{0,1:T(8,128)(2,1)S(1)}, u32[]{:S(2)}, u32[]{:S(2)}) %collective-permute-start.16) | collective-permute-done | bytes 737312 | tf_op jit(solution)/shard_map/ppermute | solution.py:31
  139.9 0.9 copy-done.3
  140.7 1.3 fusion.79
  142.1 4.0 %convolution_convert_fusion = bf16[256,1440]{0,1:T(8,128)(2,1)} fusion(bf16[360,1440]{1,0:T(8,128)(2,1)S(1)} %copy-done, f32[256,360]{0,1:T(8,128)} %fusion.79, bf16[256,1440]{0,1:T(8,128)(2,1)} %copy-done.3, bf16[1440,360]{1,0:T(8,128)(2,1)} %param.22), kind=kOutput, calls=%fused_computation | convolution fusion | flops 531947520 | bytes 3916800 | tf_op jit(solution)/shard_map/dot_general | solution.py:100
  146.2 2.5 %fusion.77 = f32[256,360]{0,1:T(8,128)} fusion(bf16[256,1440]{0,1:T(8,128)(2,1)} %collective-permute-done.13, bf16[1440,360]{1,0:T(8,128)(2,1)S(1)} %copy-done.1), kind=kOutput, calls=%fused_computation.143 | convolution fusion | flops 265420800 | bytes 2142720 | tf_op jit(solution)/shard_map/dot_general | solution.py:97
  148.6 3.9 %convolution_convert_fusion.1 = bf16[256,1440]{0,1:T(8,128)(2,1)} fusion(bf16[360,1440]{1,0:T(8,128)(2,1)S(1)} %copy-done, f32[256,360]{0,1:T(8,128)} %fusion.77, bf16[256,1440]{0,1:T(8,128)(2,1)} %collective-permute-done.13, bf16[1440,360]{1,0:T(8,128)(2,1)} %param.22), kind=kOutput, calls=%fused_computation.1 | convolution fusion | flops 531947520 | bytes 3916800 | tf_op jit(solution)/shard_map/dot_general | solution.py:100
  153.0 2.5 %fusion.78 = f32[256,360]{0,1:T(8,128)} fusion(bf16[256,1440]{0,1:T(8,128)(2,1)} %collective-permute-done.15, bf16[1440,360]{1,0:T(8,128)(2,1)S(1)} %copy-done.1), kind=kOutput, calls=%fused_computation.144 | convolution fusion | flops 265420800 | bytes 2142720 | tf_op jit(solution)/shard_map/dot_general | solution.py:97
  155.4 4.2 %add_convert_fusion.1 = bf16[256,1440]{0,1:T(8,128)(2,1)} fusion(bf16[256,1440]{0,1:T(8,128)(2,1)} %collective-permute-done.17, bf16[360,1440]{1,0:T(8,128)(2,1)S(1)} %copy-done, f32[256,360]{0,1:T(8,128)} %fusion.78, bf16[256,1440]{0,1:T(8,128)(2,1)} %collective-permute-done.15, bf16[1440,360]{1,0:T(8,128)(2,1)} %param.22), kind=kOutput, calls=%fused_computation.19 | convolution fusion | flops 532684800 | bytes 4654080 | tf_op jit(solution)/shard_map/dot_general | solution.py:100
  159.9 1.3 fusion.76
  161.2 4.0 %fusion.12 = f32[256,1440]{0,1:T(8,128)} fusion(bf16[360,1440]{1,0:T(8,128)(2,1)S(1)} %copy-done, bf16[256,1440]{1,0:T(8,128)(2,1)S(1)} %bitcast.135, bf16[1440,360]{1,0:T(8,128)(2,1)} %param.22, f32[256,360]{0,1:T(8,128)} %fusion.76), kind=kOutput, calls=%fused_computation.29 | convolution fusion | flops 531578880 | bytes 4654080 | tf_op jit(solution)/shard_map/dot_general | solution.py:100
  165.2 13.2 %collective-permute-done.18 = bf16[256,1440]{0,1:T(8,128)(2,1)} collective-permute-done((bf16[256,1440]{0,1:T(8,128)(2,1)}, bf16[256,1440]{0,1:T(8,128)(2,1)}, u32[]{:S(2)}, u32[]{:S(2)}) %collective-permute-start.18) | collective-permute-done | bytes 737312 | tf_op jit(solution)/shard_map/ppermute | solution.py:31
  178.5 2.0 add_convert_fusion
  180.7 23.9 %all_to_all.22 = bf16[8,1,32,1440]{3,2,1,0:T(8,128)(2,1)S(1)} all-to-all(bf16[8,1,32,1440]{3,2,1,0:T(8,128)(2,1)S(1)} %bitcast.138), channel_id=1, replica_groups=mesh['ctx'=4,'exp'=8] {'exp'}, dimensions={0} | all-to-all | bytes 1474560 | tf_op jit(solution)/shard_map/all_to_all | solution.py:172
  204.7 0.9 copy.84
  205.6 3.6 %all-to-all-start.3 = ((bf16[2,4,32,1440]{3,2,0,1:T(8,128)(2,1)}), bf16[2,4,32,1440]{3,2,0,1:T(8,128)(2,1)S(1)}, u32[]{:S(2)}, u32[]{:S(2)}) async-start(bf16[2,4,32,1440]{3,2,0,1:T(8,128)(2,1)} %copy.84), calls=%async_computation.3 | async-start | bytes 1572864 | tf_op jit(solution)/shard_map/all_to_all | solution.py:179
  209.4 10.6 %all-to-all-done.3 = bf16[2,4,32,1440]{3,2,0,1:T(8,128)(2,1)S(1)} async-done(((bf16[2,4,32,1440]{3,2,0,1:T(8,128)(2,1)}), bf16[2,4,32,1440]{3,2,0,1:T(8,128)(2,1)S(1)}, u32[]{:S(2)}, u32[]{:S(2)}) %all-to-all-start.3) | async-done | bytes 737312 | tf_op jit(solution)/shard_map/all_to_all | solution.py:179
  220.0 1.2 fusion.5
  (72 shorter events, 8.6 us)
Async XLA Ops:
  0.0 142.1 %copy-start = (bf16[360,1440]{1,0:T(8,128)(2,1)S(1)}, bf16[360,1440]{1,0:T(8,128)(2,1)}, u32[]{:S(2)}) copy-start(bf16[360,1440]{1,0:T(8,128)(2,1)} %param.23) | copy-start | bytes 3110404
  0.0 11.2 %copy-start.8 = (f32[32]{0:T(128)S(1)}, f32[32]{0:T(128)}, u32[]{:S(2)}) copy-start(f32[32]{0:T(128)} %param.16) | copy-start | bytes 388
  0.0 11.3 %copy-start.6 = (s32[1,64,4]{1,2,0:T(4,128)S(1)}, s32[1,64,4]{1,2,0:T(4,128)}, u32[]{:S(2)}) copy-start(s32[1,64,4]{1,2,0:T(4,128)} %param.19) | copy-start | bytes 3076
  1.7 15.8 %copy-start.9 = (s32[1,64]{1,0:T(1,128)S(1)}, s32[1,64]{1,0:T(1,128)}, u32[]{:S(2)}) copy-start(s32[1,64]{1,0:T(1,128)} %param.14) | copy-start | bytes 772
  2.5 9.6 %collective-permute-start = (bf16[64,640]{0,1:T(8,128)(2,1)}, bf16[64,640]{0,1:T(8,128)(2,1)S(1)}, u32[]{:S(2)}, u32[]{:S(2)}) collective-permute-start(bf16[64,640]{0,1:T(8,128)(2,1)} %pad_maximum_fusion), channel_id=1, source_target_pairs={{0,8},{8,16},{16,24},{24,0},{1,9},{9,17},{17,25},{25,1},{2,10},{10... | collective-permute-start | bytes 245768 | tf_op jit(solution)/shard_map/ppermute | solution.py:21
  5.4 11.3 %collective-permute-start.1 = (bf16[64,640]{0,1:T(8,128)(2,1)}, bf16[64,640]{0,1:T(8,128)(2,1)}, u32[]{:S(2)}, u32[]{:S(2)}) collective-permute-start(bf16[64,640]{0,1:T(8,128)(2,1)} %pad_maximum_fusion), channel_id=1, source_target_pairs={{0,16},{8,24},{16,0},{24,8},{1,17},{9,25},{17,1},{25,9},{2,18},{10... | collective-permute-start | bytes 245768 | tf_op jit(solution)/shard_map/ppermute | solution.py:21
  6.9 9.8 %collective-permute-start.2 = (bf16[64,640]{0,1:T(8,128)(2,1)}, bf16[64,640]{0,1:T(8,128)(2,1)}, u32[]{:S(2)}, u32[]{:S(2)}) collective-permute-start(bf16[64,640]{0,1:T(8,128)(2,1)} %pad_maximum_fusion), channel_id=1, source_target_pairs={{0,24},{8,0},{16,8},{24,16},{1,25},{9,1},{17,9},{25,17},{2,26},{10... | collective-permute-start | bytes 245768 | tf_op jit(solution)/shard_map/ppermute | solution.py:21
  8.4 42.4 %collective-permute-start.3 = (bf16[256,1440]{0,1:T(8,128)(2,1)}, bf16[256,1440]{0,1:T(8,128)(2,1)}, u32[]{:S(2)}, u32[]{:S(2)}) collective-permute-start(bf16[256,1440]{0,1:T(8,128)(2,1)} %param.17), channel_id=1, source_target_pairs={{0,1},{1,0},{2,3},{3,2},{4,5},{5,4},{6,7},{7,6},{8,9},{9,8},{10,11... | collective-permute-start | bytes 2211848 | tf_op jit(solution)/shard_map/ppermute | solution.py:31
  8.4 21.0 %collective-permute-start.5 = (bf16[256,1440]{0,1:T(8,128)(2,1)}, bf16[256,1440]{0,1:T(8,128)(2,1)S(1)}, u32[]{:S(2)}, u32[]{:S(2)}) collective-permute-start(bf16[256,1440]{0,1:T(8,128)(2,1)} %param.17), channel_id=1, source_target_pairs={{2,0},{3,1},{4,2},{5,3},{6,4},{7,5},{10,8},{11,9},{12,10},{13,11},... | collective-permute-start | bytes 2211848 | tf_op jit(solution)/shard_map/ppermute | solution.py:79
  12.1 21.0 %collective-permute-start.4 = (bf16[256,1440]{0,1:T(8,128)(2,1)}, bf16[256,1440]{0,1:T(8,128)(2,1)S(1)}, u32[]{:S(2)}, u32[]{:S(2)}) collective-permute-start(bf16[256,1440]{0,1:T(8,128)(2,1)} %param.17), channel_id=1, source_target_pairs={{0,2},{1,3},{2,4},{3,5},{4,6},{5,7},{8,10},{9,11},{10,12},{11,13},... | collective-permute-start | bytes 2211848 | tf_op jit(solution)/shard_map/ppermute | solution.py:79
  29.4 20.1 %collective-permute-start.6 = (bf16[256,1440]{0,1:T(8,128)(2,1)S(1)}, bf16[256,1440]{0,1:T(8,128)(2,1)}, u32[]{:S(2)}, u32[]{:S(2)}) collective-permute-start(bf16[256,1440]{0,1:T(8,128)(2,1)S(1)} %collective-permute-done.5), channel_id=1, source_target_pairs={{2,0},{3,1},{4,2},{5,3},{6,4},{7,5},{10,8},{11,9},{12,10},{13,11},... | collective-permute-start | bytes 2211848 | tf_op jit(solution)/shard_map/ppermute | solution.py:79
  32.2 6.4 %copy-start.2 = (bf16[256,1440]{0,1:T(8,128)(2,1)S(1)}, bf16[256,1440]{0,1:T(8,128)(2,1)}, u32[]{:S(2)}) copy-start(bf16[256,1440]{0,1:T(8,128)(2,1)} %param.17) | copy-start | bytes 2211844
  33.1 19.6 %collective-permute-start.9 = (bf16[256,1440]{0,1:T(8,128)(2,1)S(1)}, bf16[256,1440]{0,1:T(8,128)(2,1)S(1)}, u32[]{:S(2)}, u32[]{:S(2)}) collective-permute-start(bf16[256,1440]{0,1:T(8,128)(2,1)S(1)} %collective-permute-done.4), channel_id=1, source_target_pairs={{0,2},{1,3},{2,4},{3,5},{4,6},{5,7},{8,10},{9,11},{10,12},{11,13},... | collective-permute-start | bytes 2211848 | tf_op jit(solution)/shard_map/ppermute | solution.py:79
  49.5 19.3 %collective-permute-start.7 = (bf16[256,1440]{0,1:T(8,128)(2,1)}, bf16[256,1440]{0,1:T(8,128)(2,1)S(1)}, u32[]{:S(2)}, u32[]{:S(2)}) collective-permute-start(bf16[256,1440]{0,1:T(8,128)(2,1)} %collective-permute-done.6), channel_id=1, source_target_pairs={{2,0},{3,1},{4,2},{5,3},{6,4},{7,5},{10,8},{11,9},{12,10},{13,11},... | collective-permute-start | bytes 2211848 | tf_op jit(solution)/shard_map/ppermute | solution.py:79
  52.7 18.8 %collective-permute-start.11 = (bf16[256,1440]{0,1:T(8,128)(2,1)S(1)}, bf16[256,1440]{0,1:T(8,128)(2,1)S(1)}, u32[]{:S(2)}, u32[]{:S(2)}) collective-permute-start(bf16[256,1440]{0,1:T(8,128)(2,1)S(1)} %collective-permute-done.9), channel_id=1, source_target_pairs={{0,2},{1,3},{2,4},{3,5},{4,6},{5,7},{8,10},{9,11},{10,12},{11,13},... | collective-permute-start | bytes 2211848 | tf_op jit(solution)/shard_map/ppermute | solution.py:79
  58.3 13.2 %collective-permute-start.10 = (bf16[256,1440]{0,1:T(8,128)(2,1)S(1)}, bf16[256,1440]{0,1:T(8,128)(2,1)S(1)}, u32[]{:S(2)}, u32[]{:S(2)}) collective-permute-start(bf16[256,1440]{0,1:T(8,128)(2,1)S(1)} %broadcast_select_fusion.1), channel_id=1, source_target_pairs={{0,1},{1,0},{2,3},{3,2},{4,5},{5,4},{6,7},{7,6},{8,9},{9,8},{10,11... | collective-permute-start | bytes 2211848 | tf_op jit(solution)/shard_map/ppermute | solution.py:31
  68.9 3.1 %collective-permute-start.8 = (bf16[256,1440]{0,1:T(8,128)(2,1)S(1)}, bf16[256,1440]{0,1:T(8,128)(2,1)S(1)}, u32[]{:S(2)}, u32[]{:S(2)}) collective-permute-start(bf16[256,1440]{0,1:T(8,128)(2,1)S(1)} %broadcast_select_fusion.2), channel_id=1, source_target_pairs={{0,1},{1,0},{2,3},{3,2},{4,5},{5,4},{6,7},{7,6},{8,9},{9,8},{10,11... | collective-permute-start | bytes 2211848 | tf_op jit(solution)/shard_map/ppermute | solution.py:31
  71.5 2.3 %collective-permute-start.12 = (bf16[256,1440]{0,1:T(8,128)(2,1)S(1)}, bf16[256,1440]{0,1:T(8,128)(2,1)S(1)}, u32[]{:S(2)}, u32[]{:S(2)}) collective-permute-start(bf16[256,1440]{0,1:T(8,128)(2,1)S(1)} %broadcast_select_fusion), channel_id=1, source_target_pairs={{0,1},{1,0},{2,3},{3,2},{4,5},{5,4},{6,7},{7,6},{8,9},{9,8},{10,11... | collective-permute-start | bytes 2211848 | tf_op jit(solution)/shard_map/ppermute | solution.py:31
  72.7 1.5 copy-start.4
  74.2 0.7 copy-start.5
  117.1 23.6 %copy-start.1 = (bf16[1440,360]{1,0:T(8,128)(2,1)S(1)}, bf16[1440,360]{1,0:T(8,128)(2,1)}, u32[]{:S(2)}) copy-start(bf16[1440,360]{1,0:T(8,128)(2,1)} %param.21) | copy-start | bytes 3110404
  118.2 18.2 %collective-permute-start.15 = (bf16[256,1440]{0,1:T(8,128)(2,1)}, bf16[256,1440]{0,1:T(8,128)(2,1)}, u32[]{:S(2)}, u32[]{:S(2)}) collective-permute-start(bf16[256,1440]{0,1:T(8,128)(2,1)} %copy.80), channel_id=1, source_target_pairs={{0,2},{2,0},{1,3},{3,1},{4,6},{6,4},{5,7},{7,5},{8,10},{10,8},{9,1... | collective-permute-start | bytes 2211848 | tf_op jit(solution)/shard_map/ppermute | solution.py:31
  136.4 3.4 %collective-permute-start.16 = (bf16[256,1440]{0,1:T(8,128)(2,1)}, bf16[256,1440]{0,1:T(8,128)(2,1)S(1)}, u32[]{:S(2)}, u32[]{:S(2)}) collective-permute-start(bf16[256,1440]{0,1:T(8,128)(2,1)} %collective-permute-done.15), channel_id=1, source_target_pairs={{0,1},{1,0},{2,3},{3,2},{4,5},{5,4},{6,7},{7,6},{8,9},{9,8},{10,11... | collective-permute-start | bytes 2211848 | tf_op jit(solution)/shard_map/ppermute | solution.py:31
  136.4 9.8 %collective-permute-start.13 = (bf16[256,1440]{0,1:T(8,128)(2,1)}, bf16[256,1440]{0,1:T(8,128)(2,1)}, u32[]{:S(2)}, u32[]{:S(2)}) collective-permute-start(bf16[256,1440]{0,1:T(8,128)(2,1)} %copy.80), channel_id=1, source_target_pairs={{0,1},{1,0},{2,3},{3,2},{4,5},{5,4},{6,7},{7,6},{8,9},{9,8},{10,11... | collective-permute-start | bytes 2211848 | tf_op jit(solution)/shard_map/ppermute | solution.py:31
  139.9 0.9 copy-start.3
  146.0 9.4 %collective-permute-start.17 = (bf16[256,1440]{0,1:T(8,128)(2,1)}, bf16[256,1440]{0,1:T(8,128)(2,1)}, u32[]{:S(2)}, u32[]{:S(2)}) collective-permute-start(bf16[256,1440]{0,1:T(8,128)(2,1)} %convolution_convert_fusion), channel_id=1, source_target_pairs={{0,1},{1,0},{2,3},{3,2},{4,5},{5,4},{6,7},{7,6},{8,9},{9,8},{10,11... | collective-permute-start | bytes 2211848 | tf_op jit(solution)/shard_map/ppermute | solution.py:31
  152.6 12.7 %collective-permute-start.14 = (bf16[256,1440]{0,1:T(8,128)(2,1)}, bf16[256,1440]{0,1:T(8,128)(2,1)}, u32[]{:S(2)}, u32[]{:S(2)}) collective-permute-start(bf16[256,1440]{0,1:T(8,128)(2,1)} %convolution_convert_fusion.1), channel_id=1, source_target_pairs={{0,1},{1,0},{2,3},{3,2},{4,5},{5,4},{6,7},{7,6},{8,9},{9,8},{10,11... | collective-permute-start | bytes 2211848 | tf_op jit(solution)/shard_map/ppermute | solution.py:31
  159.6 18.8 %collective-permute-start.18 = (bf16[256,1440]{0,1:T(8,128)(2,1)}, bf16[256,1440]{0,1:T(8,128)(2,1)}, u32[]{:S(2)}, u32[]{:S(2)}) collective-permute-start(bf16[256,1440]{0,1:T(8,128)(2,1)} %add_convert_fusion.1), channel_id=1, source_target_pairs={{0,2},{2,0},{1,3},{3,1},{4,6},{6,4},{5,7},{7,5},{8,10},{10,8},{9,1... | collective-permute-start | bytes 2211848 | tf_op jit(solution)/shard_map/ppermute | solution.py:31
  205.6 3.6 %copy-start.7 = (f32[1,64,4]{1,2,0:T(4,128)S(1)}, f32[1,64,4]{1,2,0:T(4,128)}, u32[]{:S(2)}) copy-start(f32[1,64,4]{1,2,0:T(4,128)} %param.20) | copy-start | bytes 3076
  205.6 14.3 %all-to-all-start.3 = ((bf16[2,4,32,1440]{3,2,0,1:T(8,128)(2,1)}), bf16[2,4,32,1440]{3,2,0,1:T(8,128)(2,1)S(1)}, u32[]{:S(2)}, u32[]{:S(2)}) async-start(bf16[2,4,32,1440]{3,2,0,1:T(8,128)(2,1)} %copy.84), calls=%async_computation.3 | async-start | bytes 1572864 | tf_op jit(solution)/shard_map/all_to_all | solution.py:179

commit v3 on v2

--- a/solution.py
+++ b/solution.py
@@ -162,9 +162,11 @@
     near = held.reshape(-1, D)
     near_core = from_partner(near, "exp", 0)
     far = from_partner(near, "exp", 1)
+    out_near = ffn(near)
+    out_near_core = ffn(near_core).astype(jnp.bfloat16)
+    far, out_near, out_near_core = lax.optimization_barrier((far, out_near, out_near_core))
     far_core = from_partner(far, "exp", 0)
-    out_near = ffn(near)
-    back_near = from_partner(ffn(near_core).astype(jnp.bfloat16), "exp", 0)
+    back_near = from_partner(out_near_core, "exp", 0)
     back_far = from_partner(ffn(far_core).astype(jnp.bfloat16), "exp", 0)
     sum_far = (ffn(far) + back_far.astype(jnp.float32)).astype(jnp.bfloat16)
     returned_far = from_partner(sum_far, "exp", 1)

time: 222 us -> 214 us (0.964)
  waiting for transfers between devices: 79.5 us -> 73.2 us
    ppermute x10, waiting for transfers between devices: 35.1 us -> 28.8 us  [from_partner(): return lax.ppermute(block, axis, route)]
  transfers between devices with their start and end apart: 20 -> 20, of which waited for: 11 -> 11; matrix products, arithmetic and copies ran while one was open for 17% -> 14% of each run, Pallas kernels for 0% -> 0%
where the time goes in v3:
time: 214 us; the launch traced here: 213 us
  waiting for transfers between devices  73.2 us (34%)
  blocking collectives  64.8 us (30%)
  matrix products  29.9 us (14%)
  starting transfers between devices  27.7 us (13%)
  other arithmetic  8.5 us (4%)
  local copies, waits for them, and re-layouts  8.28 us (4%)
    ppermute x6, waiting for transfers between devices, to_next_chip(): return lax.ppermute(block, 'exp', route)  33.9 us
    ppermute x10, waiting for transfers between devices, from_partner(): return lax.ppermute(block, axis, route)  28.8 us
    all_to_all x1, blocking collectives, body(): lax.all_to_all(pieces, 'exp', split_axis=0, concat_axis=0, tiled=True)  27.1 us
    all_to_all x1, blocking collectives, body(): lax.all_to_all(result.astype(jnp.bfloat16).reshape(held.shape), 'exp', sp...  23.4 us
    ppermute x6, starting transfers between devices, to_next_chip(): return lax.ppermute(block, 'exp', route)  17.2 us
    dot_general x4, matrix products, feed_forward(): return jnp.dot(active, w_down, preferred_element_type=jnp.float32)  15.8 us
    all_to_all x1, blocking collectives, body(): lax.all_to_all(outgoing, 'ctx', split_axis=1, concat_axis=1, tiled=True)  14.3 us
    all_to_all x1, waiting for transfers between devices, body(): lax.all_to_all(back.reshape(per_row, n_ctx, cap, D), 'ctx', split_axis=1,...  10.6 us
  transfers between devices with their start and end apart: 20, of which 11 were waited for; matrix products, arithmetic and copies ran while one was open for 14% of the time, Pallas kernels for 0%

profile of v3, /device:TPU:0, one launch (start us, length us, event | category | flops | bytes accessed | tf_op | source)
XLA Modules:
  0.0 213.0 jit_solution(12271374581943081734)
XLA Ops:
  0.0 0.8 fusion.66
  0.8 1.0 copy.88
  1.8 0.7 pad_maximum_fusion
  2.5 2.9 %collective-permute-start = (bf16[64,640]{0,1:T(8,128)(2,1)}, bf16[64,640]{0,1:T(8,128)(2,1)S(1)}, u32[]{:S(2)}, u32[]{:S(2)}) collective-permute-start(bf16[64,640]{0,1:T(8,128)(2,1)} %pad_maximum_fusion), channel_id=1, source_target_pairs={{0,8},{8,16},{16,24},{24,0},{1,9},{9,17},{17,25},{25,1},{2,10},{10... | collective-permute-start | bytes 245768 | tf_op jit(solution)/shard_map/ppermute | solution.py:21
  5.4 1.5 collective-permute-start.1
  6.9 1.4 collective-permute-start.2
  8.4 1.3 collective-permute-start.5
  9.8 1.5 reshape_squeeze.10
  12.1 4.6 %collective-permute-start.4 = (bf16[256,1440]{0,1:T(8,128)(2,1)}, bf16[256,1440]{0,1:T(8,128)(2,1)S(1)}, u32[]{:S(2)}, u32[]{:S(2)}) collective-permute-start(bf16[256,1440]{0,1:T(8,128)(2,1)} %param.17), channel_id=1, source_target_pairs={{0,2},{1,3},{2,4},{3,5},{4,6},{5,7},{8,10},{9,11},{10,12},{11,13},... | collective-permute-start | bytes 2211848 | tf_op jit(solution)/shard_map/ppermute | solution.py:79
  16.7 0.8 fusion.63
  17.7 1.1 pad_maximum_fusion.7
  19.4 0.7 fusion.6
  20.2 9.2 %collective-permute-done.5 = bf16[256,1440]{0,1:T(8,128)(2,1)S(1)} collective-permute-done((bf16[256,1440]{0,1:T(8,128)(2,1)}, bf16[256,1440]{0,1:T(8,128)(2,1)S(1)}, u32[]{:S(2)}, u32[]{:S(2)}) %collective-permute-start.5) | collective-permute-done | bytes 737312 | tf_op jit(solution)/shard_map/ppermute | solution.py:79
  29.4 1.3 collective-permute-start.6
  30.7 0.8 fusion.9
  32.2 0.9 collective-permute-done.4
  33.1 4.3 %collective-permute-start.9 = (bf16[256,1440]{0,1:T(8,128)(2,1)S(1)}, bf16[256,1440]{0,1:T(8,128)(2,1)S(1)}, u32[]{:S(2)}, u32[]{:S(2)}) collective-permute-start(bf16[256,1440]{0,1:T(8,128)(2,1)S(1)} %collective-permute-done.4), channel_id=1, source_target_pairs={{0,2},{1,3},{2,4},{3,5},{4,6},{5,7},{8,10},{9,11},{10,12},{11,13},... | collective-permute-start | bytes 2211848 | tf_op jit(solution)/shard_map/ppermute | solution.py:79
  37.4 0.6 broadcast_select_fusion.4
  38.0 0.6 constant_dynamic-slice_fusion.1
  39.0 10.5 %collective-permute-done.6 = bf16[256,1440]{0,1:T(8,128)(2,1)} collective-permute-done((bf16[256,1440]{0,1:T(8,128)(2,1)S(1)}, bf16[256,1440]{0,1:T(8,128)(2,1)}, u32[]{:S(2)}, u32[]{:S(2)}) %collective-permute-start.6) | collective-permute-done | bytes 737312 | tf_op jit(solution)/shard_map/ppermute | solution.py:79
  49.5 1.3 collective-permute-start.7
  50.8 1.5 convolution_add_fusion.4
  52.7 4.4 %collective-permute-start.11 = (bf16[256,1440]{0,1:T(8,128)(2,1)S(1)}, bf16[256,1440]{0,1:T(8,128)(2,1)S(1)}, u32[]{:S(2)}, u32[]{:S(2)}) collective-permute-start(bf16[256,1440]{0,1:T(8,128)(2,1)S(1)} %collective-permute-done.9), channel_id=1, source_target_pairs={{0,2},{1,3},{2,4},{3,5},{4,6},{5,7},{8,10},{9,11},{10,12},{11,13},... | collective-permute-start | bytes 2211848 | tf_op jit(solution)/shard_map/ppermute | solution.py:79
  57.1 1.2 broadcast_select_fusion.1
  58.4 10.4 %collective-permute-done.7 = bf16[256,1440]{0,1:T(8,128)(2,1)S(1)} collective-permute-done((bf16[256,1440]{0,1:T(8,128)(2,1)}, bf16[256,1440]{0,1:T(8,128)(2,1)S(1)}, u32[]{:S(2)}, u32[]{:S(2)}) %collective-permute-start.7) | collective-permute-done | bytes 737312 | tf_op jit(solution)/shard_map/ppermute | solution.py:79
  69.0 2.5 %collective-permute-done.11 = bf16[256,1440]{0,1:T(8,128)(2,1)S(1)} collective-permute-done((bf16[256,1440]{0,1:T(8,128)(2,1)S(1)}, bf16[256,1440]{0,1:T(8,128)(2,1)S(1)}, u32[]{:S(2)}, u32[]{:S(2)}) %collective-permute-start.11) | collective-permute-done | bytes 737312 | tf_op jit(solution)/shard_map/ppermute | solution.py:79
  73.1 0.7 collective-permute-done.12
  75.7 14.3 %all_to_all.20 = bf16[2,4,32,1440]{3,2,0,1:T(8,128)(2,1)S(1)} all-to-all(bf16[2,4,32,1440]{3,2,0,1:T(8,128)(2,1)S(1)} %copy.77), channel_id=1, replica_groups=mesh['ctx'=4,'exp'=8] {'ctx'}, dimensions={1} | all-to-all | bytes 1474560 | tf_op jit(solution)/shard_map/all_to_all | solution.py:158
  90.1 27.1 %all_to_all.21 = bf16[8,1,32,1440]{3,2,1,0:T(8,128)(2,1)S(1)} all-to-all(bf16[8,1,32,1440]{3,2,1,0:T(8,128)(2,1)S(1)} %bitcast.137), channel_id=1, replica_groups=mesh['ctx'=4,'exp'=8] {'exp'}, dimensions={0} | all-to-all | bytes 1474560 | tf_op jit(solution)/shard_map/all_to_all | solution.py:160
  117.1 1.1 copy.80
  118.5 1.3 fusion.76
  119.8 4.0 %fusion.12 = f32[256,1440]{0,1:T(8,128)} fusion(bf16[360,1440]{1,0:T(8,128)(2,1)S(1)} %copy-done, bf16[256,1440]{1,0:T(8,128)(2,1)S(1)} %bitcast.135, bf16[1440,360]{1,0:T(8,128)(2,1)} %param.22, f32[256,360]{0,1:T(8,128)} %fusion.76), kind=kOutput, calls=%fused_computation.29 | convolution fusion | flops 531578880 | bytes 4654080 | tf_op jit(solution)/shard_map/dot_general | solution.py:100
  123.8 1.7 fusion.77
  125.5 3.9 %convolution_convert_fusion.1 = bf16[256,1440]{0,1:T(8,128)(2,1)} fusion(bf16[360,1440]{1,0:T(8,128)(2,1)S(1)} %copy-done, f32[256,360]{0,1:T(8,128)S(1)} %fusion.77, bf16[256,1440]{0,1:T(8,128)(2,1)} %collective-permute-done.14, bf16[1440,360]{1,0:T(8,128)(2,1)} %param.22), kind=kOutput, calls=%fused_computation.1 | convolution fusion | flops 531947520 | bytes 3916800 | tf_op jit(solution)/shard_map/dot_general | solution.py:100
  129.4 8.1 %collective-permute-done.13 = bf16[256,1440]{0,1:T(8,128)(2,1)} collective-permute-done((bf16[256,1440]{0,1:T(8,128)(2,1)}, bf16[256,1440]{0,1:T(8,128)(2,1)}, u32[]{:S(2)}, u32[]{:S(2)}) %collective-permute-start.13) | collective-permute-done | bytes 737312 | tf_op jit(solution)/shard_map/ppermute | solution.py:31
  137.5 2.4 %collective-permute-done.16 = bf16[256,1440]{0,1:T(8,128)(2,1)S(1)} collective-permute-done((bf16[256,1440]{0,1:T(8,128)(2,1)}, bf16[256,1440]{0,1:T(8,128)(2,1)S(1)}, u32[]{:S(2)}, u32[]{:S(2)}) %collective-permute-start.16) | collective-permute-done | bytes 737312 | tf_op jit(solution)/shard_map/ppermute | solution.py:31
  139.9 1.3 fusion.79
  141.2 3.7 %convolution_convert_fusion = bf16[256,1440]{0,1:T(8,128)(2,1)} fusion(bf16[360,1440]{1,0:T(8,128)(2,1)S(1)} %copy-done, f32[256,360]{0,1:T(8,128)} %fusion.79, bf16[256,1440]{0,1:T(8,128)(2,1)S(1)} %collective-permute-done.16, bf16[1440,360]{1,0:T(8,128)(2,1)} %param.22), kind=kOutput, calls=%fused_computation | convolution fusion | flops 531947520 | bytes 3916800 | tf_op jit(solution)/shard_map/dot_general | solution.py:100
  145.5 2.5 %fusion.78 = f32[256,360]{0,1:T(8,128)} fusion(bf16[256,1440]{0,1:T(8,128)(2,1)} %collective-permute-done.13, bf16[1440,360]{1,0:T(8,128)(2,1)S(1)} %copy-done.1), kind=kOutput, calls=%fused_computation.144 | convolution fusion | flops 265420800 | bytes 2142720 | tf_op jit(solution)/shard_map/dot_general | solution.py:97
  148.0 4.2 %add_convert_fusion.1 = bf16[256,1440]{0,1:T(8,128)(2,1)} fusion(bf16[256,1440]{0,1:T(8,128)(2,1)} %collective-permute-done.17, bf16[360,1440]{1,0:T(8,128)(2,1)S(1)} %copy-done, f32[256,360]{0,1:T(8,128)} %fusion.78, bf16[256,1440]{0,1:T(8,128)(2,1)} %collective-permute-done.13, bf16[1440,360]{1,0:T(8,128)(2,1)} %param.22), kind=kOutput, calls=%fused_computation.19 | convolution fusion | flops 532684800 | bytes 4654080 | tf_op jit(solution)/shard_map/dot_general | solution.py:100
  152.4 0.9 copy-done.2
  153.3 17.6 %collective-permute-done.18 = bf16[256,1440]{0,1:T(8,128)(2,1)S(1)} collective-permute-done((bf16[256,1440]{0,1:T(8,128)(2,1)}, bf16[256,1440]{0,1:T(8,128)(2,1)S(1)}, u32[]{:S(2)}, u32[]{:S(2)}) %collective-permute-start.18) | collective-permute-done | bytes 737312 | tf_op jit(solution)/shard_map/ppermute | solution.py:31
  170.9 1.9 add_convert_fusion
  173.0 23.4 %all_to_all.22 = bf16[8,1,32,1440]{3,2,1,0:T(8,128)(2,1)S(1)} all-to-all(bf16[8,1,32,1440]{3,2,1,0:T(8,128)(2,1)S(1)} %bitcast.138), channel_id=1, replica_groups=mesh['ctx'=4,'exp'=8] {'exp'}, dimensions={0} | all-to-all | bytes 1474560 | tf_op jit(solution)/shard_map/all_to_all | solution.py:174
  196.4 0.9 copy.84
  197.4 3.6 %all-to-all-start.3 = ((bf16[2,4,32,1440]{3,2,0,1:T(8,128)(2,1)}), bf16[2,4,32,1440]{3,2,0,1:T(8,128)(2,1)S(1)}, u32[]{:S(2)}, u32[]{:S(2)}) async-start(bf16[2,4,32,1440]{3,2,0,1:T(8,128)(2,1)} %copy.84), calls=%async_computation.3 | async-start | bytes 1572864 | tf_op jit(solution)/shard_map/all_to_all | solution.py:181
  201.1 10.6 %all-to-all-done.3 = bf16[2,4,32,1440]{3,2,0,1:T(8,128)(2,1)S(1)} async-done(((bf16[2,4,32,1440]{3,2,0,1:T(8,128)(2,1)}), bf16[2,4,32,1440]{3,2,0,1:T(8,128)(2,1)S(1)}, u32[]{:S(2)}, u32[]{:S(2)}) %all-to-all-start.3) | async-done | bytes 737312 | tf_op jit(solution)/shard_map/all_to_all | solution.py:181
  211.8 1.2 fusion.5
  (72 shorter events, 8.3 us)
Async XLA Ops:
  0.0 119.8 %copy-start = (bf16[360,1440]{1,0:T(8,128)(2,1)S(1)}, bf16[360,1440]{1,0:T(8,128)(2,1)}, u32[]{:S(2)}) copy-start(bf16[360,1440]{1,0:T(8,128)(2,1)} %param.23) | copy-start | bytes 3110404
  0.0 11.2 %copy-start.8 = (f32[32]{0:T(128)S(1)}, f32[32]{0:T(128)}, u32[]{:S(2)}) copy-start(f32[32]{0:T(128)} %param.16) | copy-start | bytes 388
  0.0 11.3 %copy-start.6 = (s32[1,64,4]{1,2,0:T(4,128)S(1)}, s32[1,64,4]{1,2,0:T(4,128)}, u32[]{:S(2)}) copy-start(s32[1,64,4]{1,2,0:T(4,128)} %param.19) | copy-start | bytes 3076
  1.7 15.8 %copy-start.9 = (s32[1,64]{1,0:T(1,128)S(1)}, s32[1,64]{1,0:T(1,128)}, u32[]{:S(2)}) copy-start(s32[1,64]{1,0:T(1,128)} %param.14) | copy-start | bytes 772
  2.5 9.6 %collective-permute-start = (bf16[64,640]{0,1:T(8,128)(2,1)}, bf16[64,640]{0,1:T(8,128)(2,1)S(1)}, u32[]{:S(2)}, u32[]{:S(2)}) collective-permute-start(bf16[64,640]{0,1:T(8,128)(2,1)} %pad_maximum_fusion), channel_id=1, source_target_pairs={{0,8},{8,16},{16,24},{24,0},{1,9},{9,17},{17,25},{25,1},{2,10},{10... | collective-permute-start | bytes 245768 | tf_op jit(solution)/shard_map/ppermute | solution.py:21
  5.4 11.3 %collective-permute-start.1 = (bf16[64,640]{0,1:T(8,128)(2,1)}, bf16[64,640]{0,1:T(8,128)(2,1)}, u32[]{:S(2)}, u32[]{:S(2)}) collective-permute-start(bf16[64,640]{0,1:T(8,128)(2,1)} %pad_maximum_fusion), channel_id=1, source_target_pairs={{0,16},{8,24},{16,0},{24,8},{1,17},{9,25},{17,1},{25,9},{2,18},{10... | collective-permute-start | bytes 245768 | tf_op jit(solution)/shard_map/ppermute | solution.py:21
  6.9 9.8 %collective-permute-start.2 = (bf16[64,640]{0,1:T(8,128)(2,1)}, bf16[64,640]{0,1:T(8,128)(2,1)}, u32[]{:S(2)}, u32[]{:S(2)}) collective-permute-start(bf16[64,640]{0,1:T(8,128)(2,1)} %pad_maximum_fusion), channel_id=1, source_target_pairs={{0,24},{8,0},{16,8},{24,16},{1,25},{9,1},{17,9},{25,17},{2,26},{10... | collective-permute-start | bytes 245768 | tf_op jit(solution)/shard_map/ppermute | solution.py:21
  8.4 42.4 %collective-permute-start.3 = (bf16[256,1440]{0,1:T(8,128)(2,1)}, bf16[256,1440]{0,1:T(8,128)(2,1)}, u32[]{:S(2)}, u32[]{:S(2)}) collective-permute-start(bf16[256,1440]{0,1:T(8,128)(2,1)} %param.17), channel_id=1, source_target_pairs={{0,1},{1,0},{2,3},{3,2},{4,5},{5,4},{6,7},{7,6},{8,9},{9,8},{10,11... | collective-permute-start | bytes 2211848 | tf_op jit(solution)/shard_map/ppermute | solution.py:31
  8.4 21.0 %collective-permute-start.5 = (bf16[256,1440]{0,1:T(8,128)(2,1)}, bf16[256,1440]{0,1:T(8,128)(2,1)S(1)}, u32[]{:S(2)}, u32[]{:S(2)}) collective-permute-start(bf16[256,1440]{0,1:T(8,128)(2,1)} %param.17), channel_id=1, source_target_pairs={{2,0},{3,1},{4,2},{5,3},{6,4},{7,5},{10,8},{11,9},{12,10},{13,11},... | collective-permute-start | bytes 2211848 | tf_op jit(solution)/shard_map/ppermute | solution.py:79
  12.1 21.0 %collective-permute-start.4 = (bf16[256,1440]{0,1:T(8,128)(2,1)}, bf16[256,1440]{0,1:T(8,128)(2,1)S(1)}, u32[]{:S(2)}, u32[]{:S(2)}) collective-permute-start(bf16[256,1440]{0,1:T(8,128)(2,1)} %param.17), channel_id=1, source_target_pairs={{0,2},{1,3},{2,4},{3,5},{4,6},{5,7},{8,10},{9,11},{10,12},{11,13},... | collective-permute-start | bytes 2211848 | tf_op jit(solution)/shard_map/ppermute | solution.py:79
  29.4 20.1 %collective-permute-start.6 = (bf16[256,1440]{0,1:T(8,128)(2,1)S(1)}, bf16[256,1440]{0,1:T(8,128)(2,1)}, u32[]{:S(2)}, u32[]{:S(2)}) collective-permute-start(bf16[256,1440]{0,1:T(8,128)(2,1)S(1)} %collective-permute-done.5), channel_id=1, source_target_pairs={{2,0},{3,1},{4,2},{5,3},{6,4},{7,5},{10,8},{11,9},{12,10},{13,11},... | collective-permute-start | bytes 2211848 | tf_op jit(solution)/shard_map/ppermute | solution.py:79
  32.2 6.4 %copy-start.3 = (bf16[256,1440]{0,1:T(8,128)(2,1)S(1)}, bf16[256,1440]{0,1:T(8,128)(2,1)}, u32[]{:S(2)}) copy-start(bf16[256,1440]{0,1:T(8,128)(2,1)} %param.17) | copy-start | bytes 2211844
  33.1 19.6 %collective-permute-start.9 = (bf16[256,1440]{0,1:T(8,128)(2,1)S(1)}, bf16[256,1440]{0,1:T(8,128)(2,1)S(1)}, u32[]{:S(2)}, u32[]{:S(2)}) collective-permute-start(bf16[256,1440]{0,1:T(8,128)(2,1)S(1)} %collective-permute-done.4), channel_id=1, source_target_pairs={{0,2},{1,3},{2,4},{3,5},{4,6},{5,7},{8,10},{9,11},{10,12},{11,13},... | collective-permute-start | bytes 2211848 | tf_op jit(solution)/shard_map/ppermute | solution.py:79
  49.5 19.3 %collective-permute-start.7 = (bf16[256,1440]{0,1:T(8,128)(2,1)}, bf16[256,1440]{0,1:T(8,128)(2,1)S(1)}, u32[]{:S(2)}, u32[]{:S(2)}) collective-permute-start(bf16[256,1440]{0,1:T(8,128)(2,1)} %collective-permute-done.6), channel_id=1, source_target_pairs={{2,0},{3,1},{4,2},{5,3},{6,4},{7,5},{10,8},{11,9},{12,10},{13,11},... | collective-permute-start | bytes 2211848 | tf_op jit(solution)/shard_map/ppermute | solution.py:79
  52.7 18.8 %collective-permute-start.11 = (bf16[256,1440]{0,1:T(8,128)(2,1)S(1)}, bf16[256,1440]{0,1:T(8,128)(2,1)S(1)}, u32[]{:S(2)}, u32[]{:S(2)}) collective-permute-start(bf16[256,1440]{0,1:T(8,128)(2,1)S(1)} %collective-permute-done.9), channel_id=1, source_target_pairs={{0,2},{1,3},{2,4},{3,5},{4,6},{5,7},{8,10},{9,11},{10,12},{11,13},... | collective-permute-start | bytes 2211848 | tf_op jit(solution)/shard_map/ppermute | solution.py:79
  58.3 13.2 %collective-permute-start.10 = (bf16[256,1440]{0,1:T(8,128)(2,1)S(1)}, bf16[256,1440]{0,1:T(8,128)(2,1)S(1)}, u32[]{:S(2)}, u32[]{:S(2)}) collective-permute-start(bf16[256,1440]{0,1:T(8,128)(2,1)S(1)} %broadcast_select_fusion.1), channel_id=1, source_target_pairs={{0,1},{1,0},{2,3},{3,2},{4,5},{5,4},{6,7},{7,6},{8,9},{9,8},{10,11... | collective-permute-start | bytes 2211848 | tf_op jit(solution)/shard_map/ppermute | solution.py:31
  68.9 3.1 %collective-permute-start.8 = (bf16[256,1440]{0,1:T(8,128)(2,1)S(1)}, bf16[256,1440]{0,1:T(8,128)(2,1)S(1)}, u32[]{:S(2)}, u32[]{:S(2)}) collective-permute-start(bf16[256,1440]{0,1:T(8,128)(2,1)S(1)} %broadcast_select_fusion.2), channel_id=1, source_target_pairs={{0,1},{1,0},{2,3},{3,2},{4,5},{5,4},{6,7},{7,6},{8,9},{9,8},{10,11... | collective-permute-start | bytes 2211848 | tf_op jit(solution)/shard_map/ppermute | solution.py:31
  71.5 2.3 %collective-permute-start.12 = (bf16[256,1440]{0,1:T(8,128)(2,1)S(1)}, bf16[256,1440]{0,1:T(8,128)(2,1)S(1)}, u32[]{:S(2)}, u32[]{:S(2)}) collective-permute-start(bf16[256,1440]{0,1:T(8,128)(2,1)S(1)} %broadcast_select_fusion), channel_id=1, source_target_pairs={{0,1},{1,0},{2,3},{3,2},{4,5},{5,4},{6,7},{7,6},{8,9},{9,8},{10,11... | collective-permute-start | bytes 2211848 | tf_op jit(solution)/shard_map/ppermute | solution.py:31
  72.7 1.5 copy-start.4
  74.2 0.7 copy-start.5
  117.1 1.3 copy-start.1
  118.3 5.5 %collective-permute-start.14 = (bf16[256,1440]{0,1:T(8,128)(2,1)}, bf16[256,1440]{0,1:T(8,128)(2,1)}, u32[]{:S(2)}, u32[]{:S(2)}) collective-permute-start(bf16[256,1440]{0,1:T(8,128)(2,1)} %copy.80), channel_id=1, source_target_pairs={{0,1},{1,0},{2,3},{3,2},{4,5},{5,4},{6,7},{7,6},{8,9},{9,8},{10,11... | collective-permute-start | bytes 2211848 | tf_op jit(solution)/shard_map/ppermute | solution.py:31
  118.3 19.2 %collective-permute-start.13 = (bf16[256,1440]{0,1:T(8,128)(2,1)}, bf16[256,1440]{0,1:T(8,128)(2,1)}, u32[]{:S(2)}, u32[]{:S(2)}) collective-permute-start(bf16[256,1440]{0,1:T(8,128)(2,1)} %copy.80), channel_id=1, source_target_pairs={{0,2},{2,0},{1,3},{3,1},{4,6},{6,4},{5,7},{7,5},{8,10},{10,8},{9,1... | collective-permute-start | bytes 2211848 | tf_op jit(solution)/shard_map/ppermute | solution.py:31
  137.5 2.4 %collective-permute-start.16 = (bf16[256,1440]{0,1:T(8,128)(2,1)}, bf16[256,1440]{0,1:T(8,128)(2,1)S(1)}, u32[]{:S(2)}, u32[]{:S(2)}) collective-permute-start(bf16[256,1440]{0,1:T(8,128)(2,1)} %collective-permute-done.13), channel_id=1, source_target_pairs={{0,1},{1,0},{2,3},{3,2},{4,5},{5,4},{6,7},{7,6},{8,9},{9,8},{10,11... | collective-permute-start | bytes 2211848 | tf_op jit(solution)/shard_map/ppermute | solution.py:31
  145.0 3.0 %collective-permute-start.17 = (bf16[256,1440]{0,1:T(8,128)(2,1)}, bf16[256,1440]{0,1:T(8,128)(2,1)}, u32[]{:S(2)}, u32[]{:S(2)}) collective-permute-start(bf16[256,1440]{0,1:T(8,128)(2,1)} %convolution_convert_fusion), channel_id=1, source_target_pairs={{0,1},{1,0},{2,3},{3,2},{4,5},{5,4},{6,7},{7,6},{8,9},{9,8},{10,11... | collective-permute-start | bytes 2211848 | tf_op jit(solution)/shard_map/ppermute | solution.py:31
  145.1 7.3 %collective-permute-start.15 = (bf16[256,1440]{0,1:T(8,128)(2,1)}, bf16[256,1440]{0,1:T(8,128)(2,1)S(1)}, u32[]{:S(2)}, u32[]{:S(2)}) collective-permute-start(bf16[256,1440]{0,1:T(8,128)(2,1)} %convolution_convert_fusion.1), channel_id=1, source_target_pairs={{0,1},{1,0},{2,3},{3,2},{4,5},{5,4},{6,7},{7,6},{8,9},{9,8},{10,11... | collective-permute-start | bytes 2211848 | tf_op jit(solution)/shard_map/ppermute | solution.py:31
  152.1 18.7 %collective-permute-start.18 = (bf16[256,1440]{0,1:T(8,128)(2,1)}, bf16[256,1440]{0,1:T(8,128)(2,1)S(1)}, u32[]{:S(2)}, u32[]{:S(2)}) collective-permute-start(bf16[256,1440]{0,1:T(8,128)(2,1)} %add_convert_fusion.1), channel_id=1, source_target_pairs={{0,2},{2,0},{1,3},{3,1},{4,6},{6,4},{5,7},{7,5},{8,10},{10,8},{9,1... | collective-permute-start | bytes 2211848 | tf_op jit(solution)/shard_map/ppermute | solution.py:31
  152.4 0.9 copy-start.2
  197.4 3.6 %copy-start.7 = (f32[1,64,4]{1,2,0:T(4,128)S(1)}, f32[1,64,4]{1,2,0:T(4,128)}, u32[]{:S(2)}) copy-start(f32[1,64,4]{1,2,0:T(4,128)} %param.20) | copy-start | bytes 3076
  197.4 14.3 %all-to-all-start.3 = ((bf16[2,4,32,1440]{3,2,0,1:T(8,128)(2,1)}), bf16[2,4,32,1440]{3,2,0,1:T(8,128)(2,1)S(1)}, u32[]{:S(2)}, u32[]{:S(2)}) async-start(bf16[2,4,32,1440]{3,2,0,1:T(8,128)(2,1)} %copy.84), calls=%async_computation.3 | async-start | bytes 1572864 | tf_op jit(solution)/shard_map/all_to_all | solution.py:181
